TPU v7x, 1024 devices: a whole 4x4x32 slice. The times are simulated.
1024 devices in a mesh: dom: 128 (over z, x), repl: 8 (over y, core).
Axes of the slice: x: 4, y: 4, z: 32, core: 2. Of those that a mesh axis runs over, the one named last changes fastest.
Arguments:
- features: bfloat16 [262144, 128], P(('dom', 'repl')), may hold values from -6 to 6
- weight: bfloat16 [128, 128], replicated, may hold values from -0.5 to 0.5
- grad_out: bfloat16 [262144, 128], P(('dom', 'repl')), may hold values from -6 to 6
- tile_values: bfloat16 [128, 8, 24, 256, 256], P('dom', 'repl'), may hold values from -0.09375 to 0.09375
- tile_rows: int32 [128, 8, 24], P('dom', 'repl'), may hold values from 0 to 7
- tile_cols: int32 [128, 8, 24], P('dom', 'repl'), may hold values from 0 to 4
- tile_count: int32 [128, 8], P('dom', 'repl'), may hold values from 1 to 24, as said below
Outputs:
- projected: bfloat16 [262144, 128], P(('dom', 'repl'))
- grad_features: bfloat16 [262144, 128], P(('dom', 'repl'))
Inputs may be any that keep to these rules, and one draw needn't show every extreme that they name: `tile_count`: some device has all 24 slots live.
All inputs are finite; a program needn't handle non-finite values.
Results may differ from a plain program's by a relative error of at most 0.017.
Values may be sent and summed in bfloat16 or wider, within the bound.
No kernel may reach another device: no remote copies, remote signals or barrier semaphores. Data moves between devices by JAX's collectives and lax.ppermute only.
A program may use at most 32 MiB of HBM per device.

v0:
```python
import jax
import jax.numpy as jnp
from jax import lax
from jax.sharding import PartitionSpec as P

REACH = 2


def shifted(array, axis, by):
    devices = lax.axis_size(axis)
    pairs = [(i, i + by) for i in range(devices) if 0 <= i + by < devices]
    return lax.ppermute(array, axis, pairs)


def body(features, weight, grad_out, tile_values, tile_rows, tile_cols, tile_count):
    slot_total = tile_values.shape[2]
    tile_edge = tile_values.shape[3]
    blocks_here = lax.axis_size("repl")
    spread = 2 * REACH + 1
    values = tile_values.reshape(slot_total, tile_edge, tile_edge)
    row_index = tile_rows.reshape(slot_total)
    col_index = tile_cols.reshape(slot_total)
    is_live = jnp.arange(slot_total, dtype=jnp.int32) < tile_count.reshape(())
    row_onehot = jnp.where(
        (row_index[None, :] == jnp.arange(blocks_here, dtype=jnp.int32)[:, None])
        & is_live[None, :],
        1.0,
        0.0,
    ).astype(jnp.float32)
    col_onehot = jnp.where(
        (col_index[None, :] == jnp.arange(spread, dtype=jnp.int32)[:, None]) & is_live[None, :],
        1.0,
        0.0,
    ).astype(jnp.float32)
    nearby = []
    for offset in range(spread):
        if offset == REACH:
            nearby.append(features)
        else:
            nearby.append(shifted(features, "dom", REACH - offset))
    stacked = jnp.stack(nearby, axis=0)
    feature_tiles = jnp.take(stacked, col_index, axis=0)
    products = jnp.einsum("sij,sjf->sif", values, feature_tiles, preferred_element_type=jnp.float32)
    partial_value = jnp.einsum("bs,sif->bif", row_onehot, products, precision=lax.Precision.HIGHEST)
    partial_value = partial_value.astype(jnp.bfloat16).reshape(
        blocks_here * tile_edge, partial_value.shape[2]
    )
    aggregated = lax.psum_scatter(partial_value, "repl", scatter_dimension=0, tiled=True).astype(
        jnp.float32
    )
    hidden = aggregated.astype(jnp.bfloat16)
    projected = jnp.dot(hidden, weight, preferred_element_type=jnp.float32).astype(jnp.bfloat16)
    grad_hidden = jnp.dot(grad_out, weight.T, preferred_element_type=jnp.float32).astype(
        jnp.bfloat16
    )
    slab_grads = lax.all_gather(grad_hidden, "repl", axis=0, tiled=True)
    slab_grads = slab_grads.reshape(blocks_here, tile_edge, slab_grads.shape[1])
    grad_tiles = jnp.take(slab_grads, row_index, axis=0)
    backward_terms = jnp.einsum(
        "sij,sif->sjf", values, grad_tiles, preferred_element_type=jnp.float32
    )
    offset_terms = jnp.einsum(
        "os,sjf->ojf", col_onehot, backward_terms, precision=lax.Precision.HIGHEST
    )
    summed = offset_terms[REACH]
    for offset in range(spread):
        if offset != REACH:
            summed = summed + shifted(
                offset_terms[offset].astype(jnp.bfloat16), "dom", offset - REACH
            ).astype(jnp.float32)
    grad_features = summed.astype(jnp.bfloat16)
    return (projected, grad_features)


def solution(mesh):
    placed = (
        P(("dom", "repl"), None),
        P(),
        P(("dom", "repl"), None),
        P("dom", "repl", None, None, None),
        P("dom", "repl", None),
        P("dom", "repl", None),
        P("dom", "repl"),
    )
    return jax.shard_map(
        body,
        mesh=mesh,
        in_specs=placed,
        out_specs=(P(("dom", "repl"), None), P(("dom", "repl"), None)),
        check_vma=False,
    )
```

profile of v0, /device:TPU:1, one launch (start us, length us, event | category | flops | bytes accessed | tf_op | source)
XLA Modules:
  0.0 129.3 jit_solution(5891649850423305597)
XLA Ops:
  7.2 6.4 %collective-permute-start = (bf16[256,128]{1,0:T(8,128)(2,1)}, bf16[256,128]{1,0:T(8,128)(2,1)}, u32[]{:S(2)}, u32[]{:S(2)}) collective-permute-start(bf16[256,128]{1,0:T(8,128)(2,1)} %param.7), channel_id=1, source_target_pairs={{0,16},{8,24},{16,32},{24,40},{32,48},{40,56},{48,64},{56,72},{64,... | collective-permute-start | bytes 196616 | tf_op jit(solution)/shard_map/ppermute | solution.py:12
  13.6 2.8 %collective-permute-start.1 = (bf16[256,128]{1,0:T(8,128)(2,1)}, bf16[256,128]{1,0:T(8,128)(2,1)}, u32[]{:S(2)}, u32[]{:S(2)}) collective-permute-start(bf16[256,128]{1,0:T(8,128)(2,1)} %param.7), channel_id=1, source_target_pairs={{0,8},{8,16},{16,24},{24,32},{32,40},{40,48},{48,56},{56,64},{64,7... | collective-permute-start | bytes 196616 | tf_op jit(solution)/shard_map/ppermute | solution.py:12
  16.4 1.3 collective-permute-start.2
  17.7 1.3 collective-permute-start.3
  22.3 1.0 convolution_convert_fusion.1
  23.3 23.1 %all_gather.3 = bf16[2048,128]{1,0:T(8,128)(2,1)} all-gather(bf16[256,128]{1,0:T(8,128)(2,1)S(1)} %convolution_convert_fusion.1), channel_id=1, replica_groups=mesh['dom'=128,'repl'=8] {'repl'}, dimensions={0}, use_global_device_ids=true | all-gather | bytes 589824 | tf_op jit(solution)/shard_map/all_gather | solution.py:56
  46.4 3.0 %gather_fusion.1 = bf16[24,256,128]{2,1,0:T(8,128)(2,1)} fusion(bf16[8,256,128]{2,1,0:T(8,128)(2,1)} %bitcast.66, s32[1024]{0:T(1024)S(1)} %pad_clamp_fusion), kind=kCustom, calls=%fused_computation.1 | custom fusion | bytes 3145824 | tf_op jit(solution)/shard_map/jit(_take)/gather | solution.py:58
  51.1 0.9 bitcast_dynamic-update-slice_fusion.1
  52.0 0.9 bitcast_dynamic-update-slice_fusion
  52.9 1.9 %gather_fusion = bf16[24,256,128]{2,1,0:T(8,128)(2,1)} fusion(bf16[5,256,128]{2,1,0:T(8,128)(2,1)S(1)} %bitcast_dynamic-update-slice_fusion, s32[1024]{0:T(1024)S(1)} %pad_clamp_fusion.1), kind=kCustom, calls=%fused_computation | custom fusion | bytes 3145824 | tf_op jit(solution)/shard_map/jit(_take)/gather | solution.py:42
  54.8 4.9 %fusion.4 = f32[24,256,128]{1,2,0:T(8,128)} fusion(bf16[1,1,24,256,256]{4,3,2,1,0:T(8,128)(2,1)S(1)} %copy-done, bf16[24,256,128]{2,1,0:T(8,128)(2,1)} %gather_fusion, pred[24]{0:T(512)(128)(4,1)S(1)} %compare_and_fusion.1), kind=kOutput, calls=%fused_computation.6 | convolution fusion | flops 403439616 | bytes 7864344 | tf_op jit(solution)/shard_map/sij,sjf->sif/dot_general | solution.py:43
  59.7 3.6 %copy.31 = f32[24,256,128]{2,0,1:T(8,128)} copy(f32[24,256,128]{1,2,0:T(8,128)} %fusion.4) | data formatting | bytes 6291456 | tf_op jit(solution)/shard_map/sij,sjf->sif/dot_general | solution.py:43
  63.3 3.5 %convolution_convert_fusion = bf16[8,256,128]{2,0,1:T(8,128)(2,1)S(1)} fusion(f32[24,256,128]{2,0,1:T(8,128)} %copy.31, s32[24]{0:T(128)S(1)} %bitcast.73, pred[24]{0:T(512)(128)(4,1)S(1)} %iota_compare_fusion.2), kind=kOutput, calls=%fused_computation.12 | convolution fusion | flops 75760192 | bytes 3670136 | tf_op jit(solution)/shard_map/bs,sif->bif/dot_general | solution.py:44
  66.8 0.9 copy.32
  67.7 3.9 %fusion.7 = f32[24,256,128]{1,2,0:T(8,128)} fusion(bf16[1,1,24,256,256]{4,3,2,1,0:T(8,128)(2,1)S(1)} %copy-done, bf16[24,256,128]{2,1,0:T(8,128)(2,1)} %gather_fusion.1, pred[24]{0:T(512)(128)(4,1)S(1)} %compare_and_fusion), kind=kOutput, calls=%fused_computation.7 | convolution fusion | flops 403439616 | bytes 7864344 | tf_op jit(solution)/shard_map/sij,sif->sjf/dot_general | solution.py:59
  71.6 3.6 %copy.34 = f32[24,256,128]{2,0,1:T(8,128)} copy(f32[24,256,128]{1,2,0:T(8,128)} %fusion.7) | data formatting | bytes 6291456 | tf_op jit(solution)/shard_map/sij,sif->sjf/dot_general | solution.py:59
  75.2 3.5 %fusion.42 = (bf16[5,256,128]{2,0,1:T(8,128)(2,1)S(1)}, f32[5,256,128]{2,0,1:T(8,128)S(1)}) fusion(f32[24,256,128]{2,0,1:T(8,128)} %copy.34, s32[24]{0:T(128)S(1)} %bitcast.74, pred[24]{0:T(512)(128)(4,1)S(1)} %iota_compare_fusion.2), kind=kOutput, calls=%fused_computation.62 | convolution fusion | flops 47350120 | bytes 4128888 | tf_op jit(solution)/shard_map/os,sjf->ojf/dot_general | solution.py:62
  79.1 1.3 collective-permute-start.4
  80.4 1.3 collective-permute-start.5
  81.7 4.9 %collective-permute-start.6 = (bf16[256,128]{1,0:T(8,128)(2,1)S(1)}, bf16[256,128]{1,0:T(8,128)(2,1)S(1)}, u32[]{:S(2)}, u32[]{:S(2)}) collective-permute-start(bf16[256,128]{1,0:T(8,128)(2,1)S(1)} %bitcast.71), channel_id=1, source_target_pairs={{0,8},{8,16},{16,24},{24,32},{32,40},{40,48},{48,56},{56,64},{64,7... | collective-permute-start | bytes 196616 | tf_op jit(solution)/shard_map/ppermute | solution.py:12
  86.7 7.0 %collective-permute-start.7 = (bf16[256,128]{1,0:T(8,128)(2,1)S(1)}, bf16[256,128]{1,0:T(8,128)(2,1)S(1)}, u32[]{:S(2)}, u32[]{:S(2)}) collective-permute-start(bf16[256,128]{1,0:T(8,128)(2,1)S(1)} %bitcast.72), channel_id=1, source_target_pairs={{0,16},{8,24},{16,32},{24,40},{32,48},{40,56},{48,64},{56,72},{64,... | collective-permute-start | bytes 196616 | tf_op jit(solution)/shard_map/ppermute | solution.py:12
  93.9 1.1 collective-permute-done.7
  95.7 25.2 %reduce-scatter.2.cloned.1.call-done = bf16[256,128]{1,0:T(8,128)(2,1)} async-done(((bf16[2048,128]{1,0:T(8,128)(2,1)}), bf16[256,128]{1,0:T(8,128)(2,1)}) %reduce-scatter.2.cloned.1.call-update) | async-done | bytes 65552 | tf_op jit(solution)/shard_map/reduce_scatter | solution.py:48
  120.8 1.6 %convolution_convert_fusion.2 = bf16[256,128]{1,0:T(8,128)(2,1)} fusion(bf16[256,128]{1,0:T(8,128)(2,1)} %reduce-scatter.2.cloned.1.call-done, bf16[128,128]{1,0:T(8,128)(2,1)S(1)} %copy-done.1), kind=kOutput, calls=%fused_computation.14 | convolution fusion | flops 8421376 | bytes 163840 | tf_op jit(solution)/shard_map/dot_general | solution.py:52
  (36 shorter events, 5.7 us)
Async XLA Ops:
  7.2 47.6 %copy-start = (bf16[1,1,24,256,256]{4,3,2,1,0:T(8,128)(2,1)S(1)}, bf16[1,1,24,256,256]{4,3,2,1,0:T(8,128)(2,1)}, u32[]{:S(2)}) copy-start(bf16[1,1,24,256,256]{4,3,2,1,0:T(8,128)(2,1)} %param.10) | copy-start | bytes 9437188
  7.2 43.9 %copy-start.2 = (bf16[256,128]{1,0:T(8,128)(2,1)S(1)}, bf16[256,128]{1,0:T(8,128)(2,1)}, u32[]{:S(2)}) copy-start(bf16[256,128]{1,0:T(8,128)(2,1)} %param.7) | copy-start | bytes 196612
  7.2 113.6 %reduce-scatter.2.cloned.1.call-start = ((), (), s32[]{:S(2)}) async-start(), calls=%async_computation.1 | async-start | bytes 589824 | tf_op jit(solution)/shard_map/reduce_scatter | solution.py:48
  7.2 42.2 %collective-permute-start = (bf16[256,128]{1,0:T(8,128)(2,1)}, bf16[256,128]{1,0:T(8,128)(2,1)}, u32[]{:S(2)}, u32[]{:S(2)}) collective-permute-start(bf16[256,128]{1,0:T(8,128)(2,1)} %param.7), channel_id=1, source_target_pairs={{0,16},{8,24},{16,32},{24,40},{32,48},{40,56},{48,64},{56,72},{64,... | collective-permute-start | bytes 196616 | tf_op jit(solution)/shard_map/ppermute | solution.py:12
  13.6 36.7 %collective-permute-start.1 = (bf16[256,128]{1,0:T(8,128)(2,1)}, bf16[256,128]{1,0:T(8,128)(2,1)}, u32[]{:S(2)}, u32[]{:S(2)}) collective-permute-start(bf16[256,128]{1,0:T(8,128)(2,1)} %param.7), channel_id=1, source_target_pairs={{0,8},{8,16},{16,24},{24,32},{32,40},{40,48},{48,56},{56,64},{64,7... | collective-permute-start | bytes 196616 | tf_op jit(solution)/shard_map/ppermute | solution.py:12
  16.4 34.7 %collective-permute-start.2 = (bf16[256,128]{1,0:T(8,128)(2,1)}, bf16[256,128]{1,0:T(8,128)(2,1)}, u32[]{:S(2)}, u32[]{:S(2)}) collective-permute-start(bf16[256,128]{1,0:T(8,128)(2,1)} %param.7), channel_id=1, source_target_pairs={{8,0},{16,8},{24,16},{32,24},{40,32},{48,40},{56,48},{64,56},{72,6... | collective-permute-start | bytes 196616 | tf_op jit(solution)/shard_map/ppermute | solution.py:12
  17.7 34.3 %collective-permute-start.3 = (bf16[256,128]{1,0:T(8,128)(2,1)}, bf16[256,128]{1,0:T(8,128)(2,1)}, u32[]{:S(2)}, u32[]{:S(2)}) collective-permute-start(bf16[256,128]{1,0:T(8,128)(2,1)} %param.7), channel_id=1, source_target_pairs={{16,0},{24,8},{32,16},{40,24},{48,32},{56,40},{64,48},{72,56},{80,... | collective-permute-start | bytes 196616 | tf_op jit(solution)/shard_map/ppermute | solution.py:12
  59.7 3.6 %copy-start.3 = (s32[1,1,24]{2,1,0:T(1,128)S(1)}, s32[1,1,24]{2,1,0:T(1,128)}, u32[]{:S(2)}) copy-start(s32[1,1,24]{2,1,0:T(1,128)} %param.11) | copy-start | bytes 292
  71.6 3.6 %copy-start.4 = (s32[1,1,24]{2,1,0:T(1,128)S(1)}, s32[1,1,24]{2,1,0:T(1,128)}, u32[]{:S(2)}) copy-start(s32[1,1,24]{2,1,0:T(1,128)} %param.12) | copy-start | bytes 292
  75.2 45.7 %copy-start.1 = (bf16[128,128]{1,0:T(8,128)(2,1)S(1)}, bf16[128,128]{1,0:T(8,128)(2,1)}, u32[]{:S(2)}) copy-start(bf16[128,128]{1,0:T(8,128)(2,1)} %param.8) | copy-start | bytes 98308
  79.1 14.7 %collective-permute-start.4 = (bf16[256,128]{1,0:T(8,128)(2,1)S(1)}, bf16[256,128]{1,0:T(8,128)(2,1)S(1)}, u32[]{:S(2)}, u32[]{:S(2)}) collective-permute-start(bf16[256,128]{1,0:T(8,128)(2,1)S(1)} %bitcast.69), channel_id=1, source_target_pairs={{16,0},{24,8},{32,16},{40,24},{48,32},{56,40},{64,48},{72,56},{80,... | collective-permute-start | bytes 196616 | tf_op jit(solution)/shard_map/ppermute | solution.py:12
  80.4 13.4 %collective-permute-start.5 = (bf16[256,128]{1,0:T(8,128)(2,1)S(1)}, bf16[256,128]{1,0:T(8,128)(2,1)S(1)}, u32[]{:S(2)}, u32[]{:S(2)}) collective-permute-start(bf16[256,128]{1,0:T(8,128)(2,1)S(1)} %bitcast.70), channel_id=1, source_target_pairs={{8,0},{16,8},{24,16},{32,24},{40,32},{48,40},{56,48},{64,56},{72,6... | collective-permute-start | bytes 196616 | tf_op jit(solution)/shard_map/ppermute | solution.py:12
  81.7 12.1 %collective-permute-start.6 = (bf16[256,128]{1,0:T(8,128)(2,1)S(1)}, bf16[256,128]{1,0:T(8,128)(2,1)S(1)}, u32[]{:S(2)}, u32[]{:S(2)}) collective-permute-start(bf16[256,128]{1,0:T(8,128)(2,1)S(1)} %bitcast.71), channel_id=1, source_target_pairs={{0,8},{8,16},{16,24},{24,32},{32,40},{40,48},{48,56},{56,64},{64,7... | collective-permute-start | bytes 196616 | tf_op jit(solution)/shard_map/ppermute | solution.py:12
  86.7 8.3 %collective-permute-start.7 = (bf16[256,128]{1,0:T(8,128)(2,1)S(1)}, bf16[256,128]{1,0:T(8,128)(2,1)S(1)}, u32[]{:S(2)}, u32[]{:S(2)}) collective-permute-start(bf16[256,128]{1,0:T(8,128)(2,1)S(1)} %bitcast.72), channel_id=1, source_target_pairs={{0,16},{8,24},{16,32},{24,40},{32,48},{40,56},{48,64},{56,72},{64,... | collective-permute-start | bytes 196616 | tf_op jit(solution)/shard_map/ppermute | solution.py:12
Sparse Core Ops, SparseCore 0:
  67.9 52.9 reduce-scatter.1
where the time goes:
time: 130 us; the launch traced here: 129 us
  starting transfers between devices  26.3 us (20%)
  waiting for transfers between devices  26.3 us (20%)
  blocking collectives  23.1 us (18%)
  matrix products  18.4 us (14%)
  local copies, waits for them, and re-layouts  17 us (13%)
  between operations  14.9 us (11%)
  other arithmetic  3.33 us (3%)
    ppermute x8, starting transfers between devices, shifted(): return lax.ppermute(array, axis, pairs)  26.3 us
    reduce_scatter x1, waiting for transfers between devices, body(): lax.psum_scatter(partial_value, 'repl', scatter_dimension=0, tiled=True)  25.2 us
    all_gather x1, blocking collectives, body(): slab_grads = lax.all_gather(grad_hidden, 'repl', axis=0, tiled=True)  23.1 us
    dot_general x1, matrix products, body(): jnp.einsum('sij,sjf->sif', values, feature_tiles, preferred_element_type=...  4.9 us
    dot_general x1, matrix products, body(): jnp.einsum('sij,sif->sjf', values, grad_tiles, preferred_element_type=jnp...  3.86 us
    dot_general x1, local copies, waits for them, and re-layouts, body(): jnp.einsum('sij,sjf->sif', values, feature_tiles, preferred_element_type=...  3.57 us
    dot_general x1, local copies, waits for them, and re-layouts, body(): jnp.einsum('sij,sif->sjf', values, grad_tiles, preferred_element_type=jnp...  3.57 us
    dot_general x1, matrix products, body(): jnp.einsum('os,sjf->ojf', col_onehot, backward_terms, precision=lax.Preci...  3.51 us
  transfers between devices with their start and end apart: 9, of which 2 were waited for; matrix products, arithmetic and copies ran while one was open for 17% of the time, Pallas kernels for 0%

commit v1 on v0

v1 whole, which is shorter than its diff:
```python
import functools

import jax
import jax.numpy as jnp
from jax import lax
from jax.experimental import pallas as pl
from jax.experimental.pallas import tpu as pltpu
from jax.sharding import PartitionSpec as P

REACH = 2
SPREAD = 2 * REACH + 1


def shifted(array, axis, by):
    devices = lax.axis_size(axis)
    pairs = [(i, i + by) for i in range(devices) if 0 <= i + by < devices]
    return lax.ppermute(array, axis, pairs)


def forward_kernel(rows, cols, count, tiles, f0, f1, f2, f3, f4, out, held, near, total, sems):
    live = count[0]
    slots = held.shape[0]

    def fetch(slot):
        return pltpu.make_async_copy(tiles.at[slot], held.at[slot], sems.at[slot])

    @pl.loop(0, live)
    def _(slot):
        fetch(slot).start()

    for offset, ref in enumerate((f0, f1, f2, f3, f4)):
        near[offset] = ref[...]
    total[...] = jnp.zeros_like(total)

    @pl.loop(0, live)
    def _(slot):
        fetch(slot).wait()
        row = rows[slot]
        total[row] += jnp.dot(held[slot], near[cols[slot]], preferred_element_type=jnp.float32)

    out[...] = total[...].astype(out.dtype)


def backward_kernel(rows, cols, count, tiles, grads, c0, c1, c2, c3, c4, held, turned, total, sems):
    live = count[0]

    def fetch(slot):
        return pltpu.make_async_copy(tiles.at[slot], held.at[slot], sems.at[slot])

    @pl.loop(0, live)
    def _(slot):
        fetch(slot).start()

    for block in range(grads.shape[0]):
        turned[block] = grads[block].T
    total[...] = jnp.zeros_like(total)

    @pl.loop(0, live)
    def _(slot):
        fetch(slot).wait()
        col = cols[slot]
        total[col] += jnp.dot(turned[rows[slot]], held[slot], preferred_element_type=jnp.float32)

    for offset, ref in enumerate((c0, c1, c2, c3, c4)):
        ref[...] = total[offset].T.astype(ref.dtype)


def project_kernel(parts, weight, out):
    total = jnp.sum(parts[...].astype(jnp.float32), axis=0)
    out[...] = jnp.dot(
        total.astype(jnp.bfloat16), weight[...], preferred_element_type=jnp.float32
    ).astype(out.dtype)


def features_kernel(c0, c1, c2, c3, c4, weight, out):
    total = c2[...]
    for ref in (c0, c1, c3, c4):
        total += ref[...].astype(jnp.float32)
    out[...] = lax.dot_general(
        total.astype(jnp.bfloat16),
        weight[...],
        (((1,), (1,)), ((), ())),
        preferred_element_type=jnp.float32,
    ).astype(out.dtype)


SMEM = pl.BlockSpec(memory_space=pltpu.SMEM)
VMEM = pl.BlockSpec(memory_space=pltpu.VMEM)
ANY = pl.BlockSpec(memory_space=pl.ANY)


def body(features, weight, grad_out, tile_values, tile_rows, tile_cols, tile_count):
    slots, edge = tile_values.shape[2], tile_values.shape[3]
    width = features.shape[1]
    blocks = lax.axis_size("repl")
    tiles = tile_values.reshape(slots, edge, edge)
    rows = tile_rows.reshape(slots)
    cols = tile_cols.reshape(slots)
    count = tile_count.reshape(1)
    block = jax.ShapeDtypeStruct((edge, width), jnp.bfloat16)

    spread_grads = jnp.broadcast_to(grad_out[None], (blocks, edge, width))
    slab_grads = lax.all_to_all(spread_grads, "repl", 0, 0, tiled=True)
    near = [
        features if offset == REACH else shifted(features, "dom", REACH - offset)
        for offset in range(SPREAD)
    ]
    flops = 2 * slots * edge * edge * width
    cost = pl.CostEstimate(flops=flops, bytes_accessed=slots * edge * edge * 2, transcendentals=0)
    partial = pl.pallas_call(
        forward_kernel,
        out_shape=jax.ShapeDtypeStruct((blocks, edge, width), jnp.bfloat16),
        in_specs=[SMEM] * 3 + [ANY] + [VMEM] * SPREAD,
        out_specs=VMEM,
        scratch_shapes=[
            pltpu.VMEM((slots, edge, edge), jnp.bfloat16),
            pltpu.VMEM((SPREAD, edge, width), jnp.bfloat16),
            pltpu.VMEM((blocks, edge, width), jnp.float32),
            pltpu.SemaphoreType.DMA((slots,)),
        ],
        cost_estimate=cost,
        name="forward",
    )(rows, cols, count, tiles, *near)
    slab_parts = lax.all_to_all(partial, "repl", 0, 0, tiled=True)
    terms = pl.pallas_call(
        backward_kernel,
        out_shape=[
            jax.ShapeDtypeStruct((edge, width), jnp.float32) if offset == REACH else block
            for offset in range(SPREAD)
        ],
        in_specs=[SMEM] * 3 + [ANY] + [VMEM],
        out_specs=[VMEM] * SPREAD,
        scratch_shapes=[
            pltpu.VMEM((slots, edge, edge), jnp.bfloat16),
            pltpu.VMEM((blocks, width, edge), jnp.bfloat16),
            pltpu.VMEM((SPREAD, width, edge), jnp.float32),
            pltpu.SemaphoreType.DMA((slots,)),
        ],
        cost_estimate=cost,
        name="backward",
    )(rows, cols, count, tiles, slab_grads)
    terms = [
        term if offset == REACH else shifted(term, "dom", offset - REACH)
        for offset, term in enumerate(terms)
    ]
    grad_features = pl.pallas_call(
        features_kernel,
        out_shape=block,
        in_specs=[VMEM] * (SPREAD + 1),
        out_specs=VMEM,
        name="features",
    )(*terms, weight)
    projected = pl.pallas_call(
        project_kernel,
        out_shape=block,
        in_specs=[VMEM] * 2,
        out_specs=VMEM,
        name="project",
    )(slab_parts, weight)
    return projected, grad_features


def solution(mesh):
    placed = (
        P(("dom", "repl"), None),
        P(),
        P(("dom", "repl"), None),
        P("dom", "repl", None, None, None),
        P("dom", "repl", None),
        P("dom", "repl", None),
        P("dom", "repl"),
    )
    return jax.shard_map(
        body,
        mesh=mesh,
        in_specs=placed,
        out_specs=(P(("dom", "repl"), None), P(("dom", "repl"), None)),
        check_vma=False,
    )
```

time: 130 us -> 70.8 us (0.54)
  the two profiles are of different devices: /device:TPU:1 before, /device:TPU:538 now
where the time goes in v1:
time: 70.8 us; the launch traced here: 70.1 us
  starting transfers between devices  47.9 us (68%)
  Pallas kernels  9.97 us (14%)
  waiting for transfers between devices  7 us (10%)
  local copies, waits for them, and re-layouts  3.77 us (5%)
  between operations  1.48 us (2%)
    ppermute x8, starting transfers between devices, shifted(): return lax.ppermute(array, axis, pairs)  36.9 us
    ppermute x8, waiting for transfers between devices, shifted(): return lax.ppermute(array, axis, pairs)  7 us
    all_to_all x1, starting transfers between devices, body(): slab_parts = lax.all_to_all(partial, 'repl', 0, 0, tiled=True)  6.27 us
    all_to_all x1, starting transfers between devices, body(): slab_grads = lax.all_to_all(spread_grads, 'repl', 0, 0, tiled=True)  4.69 us
    pallas_call x1, Pallas kernels, body(): pl.pallas_call(backward_kernel, out_shape=[jax.ShapeDtypeStruct((edge, wi...  3.17 us
    pallas_call x1, Pallas kernels, body(): pl.pallas_call(forward_kernel, out_shape=jax.ShapeDtypeStruct((blocks, ed...  3.13 us
    unnamed x20, local copies, waits for them, and re-layouts  2.07 us
    pallas_call x1, Pallas kernels, body(): pl.pallas_call(project_kernel, out_shape=block, in_specs=[VMEM] * 2, out_...  1.86 us
  transfers between devices with their start and end apart: 10, of which 2 were waited for; matrix products, arithmetic and copies ran while one was open for 0% of the time, Pallas kernels for 12%

profile of v1, /device:TPU:538, one launch (start us, length us, event | category | flops | bytes accessed | tf_op | source)
XLA Modules:
  0.0 70.1 jit_solution(17433992070797801430)
XLA Ops:
  0.6 1.7 %broadcast_in_dim.2 = bf16[8,256,128]{2,1,0:T(8,128)(2,1)} broadcast(bf16[256,128]{1,0:T(8,128)(2,1)} %param.9), dimensions={1,2} | broadcast | bytes 589824 | tf_op jit(solution)/shard_map/broadcast_in_dim | solution.py:102
  2.3 4.7 %all-to-all-start.1 = ((bf16[8,256,128]{2,1,0:T(8,128)(2,1)}), bf16[8,256,128]{2,1,0:T(8,128)(2,1)S(1)}, u32[]{:S(2)}, u32[]{:S(2)}) async-start(bf16[8,256,128]{2,1,0:T(8,128)(2,1)} %broadcast_in_dim.2), calls=%async_computation.1 | async-start | bytes 1048576 | tf_op jit(solution)/shard_map/all_to_all | solution.py:103
  7.0 4.0 %collective-permute-start = (bf16[256,128]{1,0:T(8,128)(2,1)}, bf16[256,128]{1,0:T(8,128)(2,1)S(1)}, u32[]{:S(2)}, u32[]{:S(2)}) collective-permute-start(bf16[256,128]{1,0:T(8,128)(2,1)} %f2.1), channel_id=1, source_target_pairs={{0,16},{8,24},{16,32},{24,40},{32,48},{40,56},{48,64},{56,72},{64,... | collective-permute-start | bytes 196616 | tf_op jit(solution)/shard_map/ppermute | solution.py:17
  11.1 2.2 %collective-permute-start.1 = (bf16[256,128]{1,0:T(8,128)(2,1)}, bf16[256,128]{1,0:T(8,128)(2,1)S(1)}, u32[]{:S(2)}, u32[]{:S(2)}) collective-permute-start(bf16[256,128]{1,0:T(8,128)(2,1)} %f2.1), channel_id=1, source_target_pairs={{0,8},{8,16},{16,24},{24,32},{32,40},{40,48},{48,56},{56,64},{64,7... | collective-permute-start | bytes 196616 | tf_op jit(solution)/shard_map/ppermute | solution.py:17
  13.3 3.6 %collective-permute-start.2 = (bf16[256,128]{1,0:T(8,128)(2,1)}, bf16[256,128]{1,0:T(8,128)(2,1)S(1)}, u32[]{:S(2)}, u32[]{:S(2)}) collective-permute-start(bf16[256,128]{1,0:T(8,128)(2,1)} %f2.1), channel_id=1, source_target_pairs={{8,0},{16,8},{24,16},{32,24},{40,32},{48,40},{56,48},{64,56},{72,6... | collective-permute-start | bytes 196616 | tf_op jit(solution)/shard_map/ppermute | solution.py:17
  16.9 5.5 %collective-permute-start.3 = (bf16[256,128]{1,0:T(8,128)(2,1)}, bf16[256,128]{1,0:T(8,128)(2,1)S(1)}, u32[]{:S(2)}, u32[]{:S(2)}) collective-permute-start(bf16[256,128]{1,0:T(8,128)(2,1)} %f2.1), channel_id=1, source_target_pairs={{16,0},{24,8},{32,16},{40,24},{48,32},{56,40},{64,48},{72,56},{80,... | collective-permute-start | bytes 196616 | tf_op jit(solution)/shard_map/ppermute | solution.py:17
  23.1 0.0 copy-start.2
  23.1 0.0 collective-permute-done.1.f1
  23.1 0.0 copy-start.3
  23.1 0.0 collective-permute-done.2.f3
  23.1 1.6 %collective-permute-done.3.f4 = bf16[256,128]{1,0:T(8,128)(2,1)S(1)} collective-permute-done((bf16[256,128]{1,0:T(8,128)(2,1)}, bf16[256,128]{1,0:T(8,128)(2,1)S(1)}, u32[]{:S(2)}, u32[]{:S(2)}) %collective-permute-start.3) | collective-permute-done | bytes 65568 | tf_op jit(solution)/shard_map/ppermute | solution.py:17
  24.8 0.6 copy-done.5
  25.4 3.1 %forward.1 = bf16[8,256,128]{2,1,0:T(8,128)(2,1)} custom-call(s32[24]{0:T(128)} %bitcast.8, s32[24]{0:T(128)} %bitcast.10, s32[1]{0:T(128)} %bitcast.4.count, bf16[24,256,256]{2,1,0:T(8,128)(2,1)} %bitcast.6, bf16[256,128]{1,0:T(8,128)(2,1)} %copy-done.2, bf16[256,128]{1,0:T(8,128)(2,1)} %copy-done.3, bf16[256,128]{1,0:T(8,128)(2,1)} %f2.1, ...), custom_call_target="tpu_custom_call" | custom-call | flops 402653184 | bytes 3145728 | tf_op jit(solution)/shard_map/forward/pallas_call | solution.py:110
  28.6 6.3 %all-to-all-start = ((bf16[8,256,128]{2,1,0:T(8,128)(2,1)}), bf16[8,256,128]{2,1,0:T(8,128)(2,1)S(1)}, u32[]{:S(2)}, u32[]{:S(2)}) async-start(bf16[8,256,128]{2,1,0:T(8,128)(2,1)} %forward.1), calls=%async_computation | async-start | bytes 1048576 | tf_op jit(solution)/shard_map/all_to_all | solution.py:124
  34.9 3.2 %backward.1 = (bf16[256,128]{1,0:T(8,128)(2,1)}, bf16[256,128]{1,0:T(8,128)(2,1)}, f32[256,128]{1,0:T(8,128)}, bf16[256,128]{1,0:T(8,128)(2,1)}, bf16[256,128]{1,0:T(8,128)(2,1)}) custom-call(s32[24]{0:T(128)} %bitcast.9, s32[24]{0:T(128)} %bitcast.11, s32[1]{0:T(128)} %bitcast.5.count, bf16[24,256,256]{2,1,0:T(8,128)(2,1)} %bitcast.7, ...), custom_call_target="tpu_custom_call" | custom-call | flops 402653184 | bytes 3145728 | tf_op jit(solution)/shard_map/backward/pallas_call | solution.py:125
  38.0 13.8 %collective-permute-start.4 = (bf16[256,128]{1,0:T(8,128)(2,1)}, bf16[256,128]{1,0:T(8,128)(2,1)S(1)}, u32[]{:S(2)}, u32[]{:S(2)}) collective-permute-start(bf16[256,128]{1,0:T(8,128)(2,1)} %get-tuple-element.7), channel_id=1, source_target_pairs={{16,0},{24,8},{32,16},{40,24},{48,32},{56,40},{64,48},{72,56},{80,... | collective-permute-start | bytes 196616 | tf_op jit(solution)/shard_map/ppermute | solution.py:17
  51.9 1.9 %collective-permute-start.5 = (bf16[256,128]{1,0:T(8,128)(2,1)}, bf16[256,128]{1,0:T(8,128)(2,1)S(1)}, u32[]{:S(2)}, u32[]{:S(2)}) collective-permute-start(bf16[256,128]{1,0:T(8,128)(2,1)} %get-tuple-element.8), channel_id=1, source_target_pairs={{8,0},{16,8},{24,16},{32,24},{40,32},{48,40},{56,48},{64,56},{72,6... | collective-permute-start | bytes 196616 | tf_op jit(solution)/shard_map/ppermute | solution.py:17
  53.8 3.9 %collective-permute-start.6 = (bf16[256,128]{1,0:T(8,128)(2,1)}, bf16[256,128]{1,0:T(8,128)(2,1)S(1)}, u32[]{:S(2)}, u32[]{:S(2)}) collective-permute-start(bf16[256,128]{1,0:T(8,128)(2,1)} %get-tuple-element.10), channel_id=1, source_target_pairs={{0,8},{8,16},{16,24},{24,32},{32,40},{40,48},{48,56},{56,64},{64,7... | collective-permute-start | bytes 196616 | tf_op jit(solution)/shard_map/ppermute | solution.py:17
  57.7 1.9 %collective-permute-start.7 = (bf16[256,128]{1,0:T(8,128)(2,1)}, bf16[256,128]{1,0:T(8,128)(2,1)S(1)}, u32[]{:S(2)}, u32[]{:S(2)}) collective-permute-start(bf16[256,128]{1,0:T(8,128)(2,1)} %get-tuple-element.11), channel_id=1, source_target_pairs={{0,16},{8,24},{16,32},{24,40},{32,48},{40,56},{48,64},{56,72},{64,... | collective-permute-start | bytes 196616 | tf_op jit(solution)/shard_map/ppermute | solution.py:17
  59.7 0.8 %copy-done = bf16[8,256,128]{2,1,0:T(8,128)(2,1)} copy-done((bf16[8,256,128]{2,1,0:T(8,128)(2,1)}, bf16[8,256,128]{2,1,0:T(8,128)(2,1)S(1)}, u32[]{:S(2)}) %copy-start) | copy-done | bytes 524312
  60.5 1.9 %project.1 = bf16[256,128]{1,0:T(8,128)(2,1)} custom-call(bf16[8,256,128]{2,1,0:T(8,128)(2,1)} %copy-done, bf16[128,128]{1,0:T(8,128)(2,1)} %weight.3), custom_call_target="tpu_custom_call" | custom-call | tf_op jit(solution)/shard_map/project/pallas_call | solution.py:153
  62.4 5.3 %collective-permute-done.7.c4 = bf16[256,128]{1,0:T(8,128)(2,1)S(1)} collective-permute-done((bf16[256,128]{1,0:T(8,128)(2,1)}, bf16[256,128]{1,0:T(8,128)(2,1)S(1)}, u32[]{:S(2)}, u32[]{:S(2)}) %collective-permute-start.7) | collective-permute-done | bytes 65568 | tf_op jit(solution)/shard_map/ppermute | solution.py:17
  67.7 0.6 copy-done.9
  68.3 1.8 %features.1 = bf16[256,128]{1,0:T(8,128)(2,1)} custom-call(bf16[256,128]{1,0:T(8,128)(2,1)} %copy-done.6, bf16[256,128]{1,0:T(8,128)(2,1)} %copy-done.7, f32[256,128]{1,0:T(8,128)} %get-tuple-element.9.c2, bf16[256,128]{1,0:T(8,128)(2,1)} %copy-done.8, bf16[256,128]{1,0:T(8,128)(2,1)} %copy-done.9, bf16[128,128]{1,0:T(8,128)(2,1)} %weight.3), custom_call_target="tpu_custom_call" | custom-call | tf_op jit(solution)/shard_map/features/pallas_call | solution.py:146
  (21 shorter events, 0.0 us)
Async XLA Ops:
  2.3 26.2 %all-to-all-start.1 = ((bf16[8,256,128]{2,1,0:T(8,128)(2,1)}), bf16[8,256,128]{2,1,0:T(8,128)(2,1)S(1)}, u32[]{:S(2)}, u32[]{:S(2)}) async-start(bf16[8,256,128]{2,1,0:T(8,128)(2,1)} %broadcast_in_dim.2), calls=%async_computation.1 | async-start | bytes 1048576 | tf_op jit(solution)/shard_map/all_to_all | solution.py:103
  7.0 16.1 %collective-permute-start = (bf16[256,128]{1,0:T(8,128)(2,1)}, bf16[256,128]{1,0:T(8,128)(2,1)S(1)}, u32[]{:S(2)}, u32[]{:S(2)}) collective-permute-start(bf16[256,128]{1,0:T(8,128)(2,1)} %f2.1), channel_id=1, source_target_pairs={{0,16},{8,24},{16,32},{24,40},{32,48},{40,56},{48,64},{56,72},{64,... | collective-permute-start | bytes 196616 | tf_op jit(solution)/shard_map/ppermute | solution.py:17
  11.1 12.1 %collective-permute-start.1 = (bf16[256,128]{1,0:T(8,128)(2,1)}, bf16[256,128]{1,0:T(8,128)(2,1)S(1)}, u32[]{:S(2)}, u32[]{:S(2)}) collective-permute-start(bf16[256,128]{1,0:T(8,128)(2,1)} %f2.1), channel_id=1, source_target_pairs={{0,8},{8,16},{16,24},{24,32},{32,40},{40,48},{48,56},{56,64},{64,7... | collective-permute-start | bytes 196616 | tf_op jit(solution)/shard_map/ppermute | solution.py:17
  13.3 9.8 %collective-permute-start.2 = (bf16[256,128]{1,0:T(8,128)(2,1)}, bf16[256,128]{1,0:T(8,128)(2,1)S(1)}, u32[]{:S(2)}, u32[]{:S(2)}) collective-permute-start(bf16[256,128]{1,0:T(8,128)(2,1)} %f2.1), channel_id=1, source_target_pairs={{8,0},{16,8},{24,16},{32,24},{40,32},{48,40},{56,48},{64,56},{72,6... | collective-permute-start | bytes 196616 | tf_op jit(solution)/shard_map/ppermute | solution.py:17
  16.9 7.9 %collective-permute-start.3 = (bf16[256,128]{1,0:T(8,128)(2,1)}, bf16[256,128]{1,0:T(8,128)(2,1)S(1)}, u32[]{:S(2)}, u32[]{:S(2)}) collective-permute-start(bf16[256,128]{1,0:T(8,128)(2,1)} %f2.1), channel_id=1, source_target_pairs={{16,0},{24,8},{32,16},{40,24},{48,32},{56,40},{64,48},{72,56},{80,... | collective-permute-start | bytes 196616 | tf_op jit(solution)/shard_map/ppermute | solution.py:17
  23.1 1.7 %copy-start.2 = (bf16[256,128]{1,0:T(8,128)(2,1)}, bf16[256,128]{1,0:T(8,128)(2,1)S(1)}, u32[]{:S(2)}) copy-start(bf16[256,128]{1,0:T(8,128)(2,1)S(1)} %collective-permute-done.f0) | copy-start | bytes 196612
  23.1 1.7 %copy-start.3 = (bf16[256,128]{1,0:T(8,128)(2,1)}, bf16[256,128]{1,0:T(8,128)(2,1)S(1)}, u32[]{:S(2)}) copy-start(bf16[256,128]{1,0:T(8,128)(2,1)S(1)} %collective-permute-done.1.f1) | copy-start | bytes 196612
  23.1 1.7 %copy-start.4 = (bf16[256,128]{1,0:T(8,128)(2,1)}, bf16[256,128]{1,0:T(8,128)(2,1)S(1)}, u32[]{:S(2)}) copy-start(bf16[256,128]{1,0:T(8,128)(2,1)S(1)} %collective-permute-done.2.f3) | copy-start | bytes 196612
  24.8 0.6 copy-start.5
  28.6 6.3 %copy-start.1 = (bf16[8,256,128]{2,1,0:T(8,128)(2,1)}, bf16[8,256,128]{2,1,0:T(8,128)(2,1)S(1)}, u32[]{:S(2)}) copy-start(bf16[8,256,128]{2,1,0:T(8,128)(2,1)S(1)} %all-to-all-done.1.grads) | copy-start | bytes 1572868
  28.6 31.1 %all-to-all-start = ((bf16[8,256,128]{2,1,0:T(8,128)(2,1)}), bf16[8,256,128]{2,1,0:T(8,128)(2,1)S(1)}, u32[]{:S(2)}, u32[]{:S(2)}) async-start(bf16[8,256,128]{2,1,0:T(8,128)(2,1)} %forward.1), calls=%async_computation | async-start | bytes 1048576 | tf_op jit(solution)/shard_map/all_to_all | solution.py:124
  38.0 24.3 %collective-permute-start.4 = (bf16[256,128]{1,0:T(8,128)(2,1)}, bf16[256,128]{1,0:T(8,128)(2,1)S(1)}, u32[]{:S(2)}, u32[]{:S(2)}) collective-permute-start(bf16[256,128]{1,0:T(8,128)(2,1)} %get-tuple-element.7), channel_id=1, source_target_pairs={{16,0},{24,8},{32,16},{40,24},{48,32},{56,40},{64,48},{72,56},{80,... | collective-permute-start | bytes 196616 | tf_op jit(solution)/shard_map/ppermute | solution.py:17
  51.9 10.5 %collective-permute-start.5 = (bf16[256,128]{1,0:T(8,128)(2,1)}, bf16[256,128]{1,0:T(8,128)(2,1)S(1)}, u32[]{:S(2)}, u32[]{:S(2)}) collective-permute-start(bf16[256,128]{1,0:T(8,128)(2,1)} %get-tuple-element.8), channel_id=1, source_target_pairs={{8,0},{16,8},{24,16},{32,24},{40,32},{48,40},{56,48},{64,56},{72,6... | collective-permute-start | bytes 196616 | tf_op jit(solution)/shard_map/ppermute | solution.py:17
  53.8 8.6 %collective-permute-start.6 = (bf16[256,128]{1,0:T(8,128)(2,1)}, bf16[256,128]{1,0:T(8,128)(2,1)S(1)}, u32[]{:S(2)}, u32[]{:S(2)}) collective-permute-start(bf16[256,128]{1,0:T(8,128)(2,1)} %get-tuple-element.10), channel_id=1, source_target_pairs={{0,8},{8,16},{16,24},{24,32},{32,40},{40,48},{48,56},{56,64},{64,7... | collective-permute-start | bytes 196616 | tf_op jit(solution)/shard_map/ppermute | solution.py:17
  57.7 10.0 %collective-permute-start.7 = (bf16[256,128]{1,0:T(8,128)(2,1)}, bf16[256,128]{1,0:T(8,128)(2,1)S(1)}, u32[]{:S(2)}, u32[]{:S(2)}) collective-permute-start(bf16[256,128]{1,0:T(8,128)(2,1)} %get-tuple-element.11), channel_id=1, source_target_pairs={{0,16},{8,24},{16,32},{24,40},{32,48},{40,56},{48,64},{56,72},{64,... | collective-permute-start | bytes 196616 | tf_op jit(solution)/shard_map/ppermute | solution.py:17
  59.7 0.8 %copy-start = (bf16[8,256,128]{2,1,0:T(8,128)(2,1)}, bf16[8,256,128]{2,1,0:T(8,128)(2,1)S(1)}, u32[]{:S(2)}) copy-start(bf16[8,256,128]{2,1,0:T(8,128)(2,1)S(1)} %all-to-all-done.parts) | copy-start | bytes 1572868
  62.3 5.4 %copy-start.6 = (bf16[256,128]{1,0:T(8,128)(2,1)}, bf16[256,128]{1,0:T(8,128)(2,1)S(1)}, u32[]{:S(2)}) copy-start(bf16[256,128]{1,0:T(8,128)(2,1)S(1)} %collective-permute-done.4.c0) | copy-start | bytes 196612
  62.3 5.4 %copy-start.7 = (bf16[256,128]{1,0:T(8,128)(2,1)}, bf16[256,128]{1,0:T(8,128)(2,1)S(1)}, u32[]{:S(2)}) copy-start(bf16[256,128]{1,0:T(8,128)(2,1)S(1)} %collective-permute-done.5.c1) | copy-start | bytes 196612
  62.4 5.4 %copy-start.8 = (bf16[256,128]{1,0:T(8,128)(2,1)}, bf16[256,128]{1,0:T(8,128)(2,1)S(1)}, u32[]{:S(2)}) copy-start(bf16[256,128]{1,0:T(8,128)(2,1)S(1)} %collective-permute-done.6.c3) | copy-start | bytes 196612
  67.7 0.6 copy-start.9

commit v2 on v1

v2 whole, which is shorter than its diff:
```python
import jax
import jax.numpy as jnp
from jax import lax
from jax.experimental import pallas as pl
from jax.experimental.pallas import tpu as pltpu
from jax.sharding import PartitionSpec as P

REACH = 2
SPREAD = 2 * REACH + 1
TOGETHER = 2
LIMIT = pltpu.CompilerParams(vmem_limit_bytes=16 * 2**20)

SMEM = pl.BlockSpec(memory_space=pltpu.SMEM)
VMEM = pl.BlockSpec(memory_space=pltpu.VMEM)
ANY = pl.BlockSpec(memory_space=pl.ANY)
HBM = pl.BlockSpec(memory_space=pltpu.HBM)


def in_hbm(array):
    return pltpu.with_memory_space_constraint(array, pltpu.HBM)


def shifted(array, axis, by):
    devices = lax.axis_size(axis)
    pairs = [(i, i + by) for i in range(devices) if 0 <= i + by < devices]
    return lax.ppermute(array, axis, pairs)


def spread_kernel(grads, spread, block, turned, load_sem, sems):
    load = pltpu.make_async_copy(grads, block, load_sem)
    load.start()
    load.wait()
    turned[...] = block[...].T
    copies = [
        pltpu.make_async_copy(turned, spread.at[index], sems.at[index])
        for index in range(spread.shape[0])
    ]
    for copy in copies:
        copy.start()
    for copy in copies:
        copy.wait()


def split_slots(cols, live, lists):
    def place(slot, lengths):
        even, odd = lengths
        is_odd = lax.rem(cols[slot], 2)
        lists[is_odd, jnp.where(is_odd == 1, odd, even)] = slot
        return even + 1 - is_odd, odd + is_odd

    zero = jnp.int32(0)
    return lax.fori_loop(0, live, place, (zero, zero))


def early_kernel(
    rows_from, cols_from, count_from, tiles, features, grads, below, above,
    held, up, down, ends,
    rows, cols, count, lists, back, ready, int_sems, tile_sems, block_sems, send_sems,
):
    def fetch(slot):
        return pltpu.make_async_copy(tiles.at[slot], held.at[slot], tile_sems.at[slot])

    ints = [
        pltpu.make_async_copy(source, target, int_sems.at[index])
        for index, (source, target) in enumerate(
            ((count_from, count), (rows_from, rows), (cols_from, cols))
        )
    ]
    for copy in ints:
        copy.start()
    own = [pltpu.make_async_copy(features, ends.at[1], block_sems.at[0])]
    own[0].start()
    back[...] = jnp.zeros_like(back)
    ends[0] = below[...]
    ends[2] = above[...]
    ints[0].wait()
    live = count[0]

    @pl.loop(0, live)
    def _(slot):
        fetch(slot).start()

    ints[1].wait()
    ints[2].wait()
    own[0].wait()
    own = [
        pltpu.make_async_copy(ends.at[1], target.at[1], block_sems.at[1 + index])
        for index, target in enumerate((up, down))
    ]
    for copy in own:
        copy.start()
    even, odd = split_slots(cols, live, lists)

    @pl.loop(0, lax.div(odd + TOGETHER - 1, TOGETHER))
    def _(step):
        sums = []
        slots = []
        for k in range(TOGETHER):
            place = step * TOGETHER + k
            slot = lists[1, jnp.minimum(place, odd - 1)]
            slots.append((place < odd, slot))

            @pl.when(place < odd)
            def _():
                fetch(slot).wait()

        for used, slot in slots:
            term = jnp.dot(grads[rows[slot]], held[slot], preferred_element_type=jnp.float32)
            sums.append((jnp.where(used, lax.div(cols[slot], 2), 2), term))
        for index, term in sums:
            back[index] += term

    sends = []
    for index, target in enumerate((down, up)):
        ready[index] = back[index].T.astype(ready.dtype)
        sends.append(pltpu.make_async_copy(ready.at[index], target.at[0], send_sems.at[index]))
        sends[-1].start()

    @pl.loop(0, even)
    def _(place):
        fetch(lists[0, place]).wait()

    for copy in sends + own:
        copy.wait()


def late_kernel(
    rows_from, cols_from, count_from, held, grads, ends, from_below, from_above,
    parts, far_down, far_up, kept,
    rows, cols, count, lists, near, total, back, staged, ready, sums_here, int_sems, send_sems,
):
    blocks = grads.shape[0]
    ints = [
        pltpu.make_async_copy(source, target, int_sems.at[index])
        for index, (source, target) in enumerate(
            ((count_from, count), (rows_from, rows), (cols_from, cols))
        )
    ]
    for copy in ints:
        copy.start()
    near[0] = ends[0]
    near[1] = from_below[1]
    near[2] = ends[1]
    near[3] = from_above[1]
    near[4] = ends[2]
    total[...] = jnp.zeros_like(total)
    back[...] = jnp.zeros_like(back)
    for copy in ints:
        copy.wait()
    even, odd = split_slots(cols, count[0], lists)

    def run(parity, length):
        @pl.loop(0, lax.div(length + TOGETHER - 1, TOGETHER))
        def _(step):
            sums = []
            for k in range(TOGETHER):
                place = step * TOGETHER + k
                slot = lists[parity, jnp.minimum(place, length - 1)]
                used = place < length
                row, col = rows[slot], cols[slot]
                tile = held[slot]
                ahead = jnp.dot(tile, near[col], preferred_element_type=jnp.float32)
                sums.append((total, jnp.where(used, row, blocks), ahead))
                if parity == 0:
                    behind = jnp.dot(grads[row], tile, preferred_element_type=jnp.float32)
                    sums.append((back, jnp.where(used, lax.div(col, 2), 3), behind))
            for target, index, term in sums:
                target[index] += term

    run(0, even)
    run(1, odd)

    copies = []
    for block in range(blocks):
        staged[block] = total[block].astype(staged.dtype)
        copies.append(
            pltpu.make_async_copy(staged.at[block], parts.at[block], send_sems.at[block])
        )
        copies[-1].start()
    for index, target in enumerate((far_down, far_up)):
        ready[index] = back[2 * index].astype(ready.dtype)
        copies.append(
            pltpu.make_async_copy(ready.at[index], target, send_sems.at[blocks + index])
        )
        copies[-1].start()
    sums_here[...] = (
        back[1].T + from_below[0].astype(jnp.float32) + from_above[0].astype(jnp.float32)
    )
    copies.append(pltpu.make_async_copy(sums_here, kept, send_sems.at[blocks + 2]))
    copies[-1].start()
    for copy in copies:
        copy.wait()


def project_kernel(parts, weight, kept, out, kept_out):
    total = jnp.sum(parts[...].astype(jnp.float32), axis=0)
    out[...] = jnp.dot(
        total.astype(jnp.bfloat16), weight[...], preferred_element_type=jnp.float32
    ).astype(out.dtype)
    kept_out[...] = kept[...]


def features_kernel(kept, from_below, from_above, weight, out):
    far = from_below[...].astype(jnp.float32) + from_above[...].astype(jnp.float32)
    total = kept[...] + far.T
    out[...] = lax.dot_general(
        total.astype(jnp.bfloat16),
        weight[...],
        (((1,), (1,)), ((), ())),
        preferred_element_type=jnp.float32,
    ).astype(out.dtype)


def body(features, weight, grad_out, tile_values, tile_rows, tile_cols, tile_count):
    slots, edge = tile_values.shape[2], tile_values.shape[3]
    width = features.shape[1]
    blocks = lax.axis_size("repl")
    tiles = in_hbm(tile_values.reshape(slots, edge, edge))
    ints = [
        in_hbm(tile_rows.reshape(slots)),
        in_hbm(tile_cols.reshape(slots)),
        tile_count.reshape(1),
    ]
    int_scratch = [
        pltpu.SMEM((slots,), jnp.int32),
        pltpu.SMEM((slots,), jnp.int32),
        pltpu.SMEM((1,), jnp.int32),
        pltpu.SMEM((2, slots), jnp.int32),
    ]
    flops = 2 * slots * edge * edge * width
    moved = slots * edge * edge * 2

    spread = pl.pallas_call(
        spread_kernel,
        out_shape=pltpu.HBM((blocks, width, edge), jnp.bfloat16),
        in_specs=[HBM],
        out_specs=HBM,
        scratch_shapes=[
            pltpu.VMEM((edge, width), jnp.bfloat16),
            pltpu.VMEM((width, edge), jnp.bfloat16),
            pltpu.SemaphoreType.DMA,
            pltpu.SemaphoreType.DMA((blocks,)),
        ],
        compiler_params=LIMIT,
        name="spread",
    )(in_hbm(grad_out))
    slab_grads = lax.all_to_all(spread, "repl", 0, 0, tiled=True)
    below = shifted(features, "dom", REACH)
    above = shifted(features, "dom", -REACH)
    held, up, down, ends = pl.pallas_call(
        early_kernel,
        out_shape=[
            pltpu.VMEM((slots, edge, edge), jnp.bfloat16),
            pltpu.HBM((2, edge, width), jnp.bfloat16),
            pltpu.HBM((2, edge, width), jnp.bfloat16),
            pltpu.VMEM((3, edge, width), jnp.bfloat16),
        ],
        in_specs=[HBM] * 2 + [ANY] + [HBM] * 2 + [VMEM] * 3,
        out_specs=[VMEM, HBM, HBM, VMEM],
        scratch_shapes=int_scratch
        + [
            pltpu.VMEM((3, width, edge), jnp.float32),
            pltpu.VMEM((2, edge, width), jnp.bfloat16),
            pltpu.SemaphoreType.DMA((3,)),
            pltpu.SemaphoreType.DMA((slots,)),
            pltpu.SemaphoreType.DMA((3,)),
            pltpu.SemaphoreType.DMA((2,)),
        ],
        cost_estimate=pl.CostEstimate(flops=flops, bytes_accessed=moved, transcendentals=0),
        compiler_params=LIMIT,
        name="early",
    )(*ints, tiles, in_hbm(features), slab_grads, below, above)
    from_below = shifted(up, "dom", 1)
    from_above = shifted(down, "dom", -1)
    partial, far_down, far_up, kept = pl.pallas_call(
        late_kernel,
        out_shape=[
            pltpu.HBM((blocks, edge, width), jnp.bfloat16),
            pltpu.HBM((width, edge), jnp.bfloat16),
            pltpu.HBM((width, edge), jnp.bfloat16),
            pltpu.HBM((edge, width), jnp.float32),
        ],
        in_specs=[HBM] * 2 + [ANY] + [VMEM] * 5,
        out_specs=[HBM] * 4,
        scratch_shapes=int_scratch
        + [
            pltpu.VMEM((SPREAD, edge, width), jnp.bfloat16),
            pltpu.VMEM((blocks + 1, edge, width), jnp.float32),
            pltpu.VMEM((4, width, edge), jnp.float32),
            pltpu.VMEM((blocks, edge, width), jnp.bfloat16),
            pltpu.VMEM((2, width, edge), jnp.bfloat16),
            pltpu.VMEM((edge, width), jnp.float32),
            pltpu.SemaphoreType.DMA((3,)),
            pltpu.SemaphoreType.DMA((blocks + 3,)),
        ],
        cost_estimate=pl.CostEstimate(flops=flops, bytes_accessed=moved, transcendentals=0),
        compiler_params=LIMIT,
        name="late",
    )(*ints, held, slab_grads, ends, from_below, from_above)
    slab_parts = lax.all_to_all(partial, "repl", 0, 0, tiled=True)
    far_from_above = shifted(far_down, "dom", -REACH)
    far_from_below = shifted(far_up, "dom", REACH)
    projected, kept = pl.pallas_call(
        project_kernel,
        out_shape=[
            jax.ShapeDtypeStruct((edge, width), jnp.bfloat16),
            pltpu.VMEM((edge, width), jnp.float32),
        ],
        in_specs=[VMEM] * 3,
        out_specs=[VMEM] * 2,
        compiler_params=LIMIT,
        name="project",
    )(slab_parts, weight, in_hbm(kept))
    grad_features = pl.pallas_call(
        features_kernel,
        out_shape=jax.ShapeDtypeStruct((edge, width), jnp.bfloat16),
        in_specs=[VMEM] * 4,
        out_specs=VMEM,
        compiler_params=LIMIT,
        name="features",
    )(kept, far_from_below, far_from_above, weight)
    return projected, grad_features


def solution(mesh):
    placed = (
        P(("dom", "repl"), None),
        P(),
        P(("dom", "repl"), None),
        P("dom", "repl", None, None, None),
        P("dom", "repl", None),
        P("dom", "repl", None),
        P("dom", "repl"),
    )
    return jax.shard_map(
        body,
        mesh=mesh,
        in_specs=placed,
        out_specs=(P(("dom", "repl"), None), P(("dom", "repl"), None)),
        check_vma=False,
    )
```

time: 70.8 us -> 62.2 us (0.88)
  the two profiles are of different devices: /device:TPU:538 before, /device:TPU:1 now
where the time goes in v2:
time: 62.2 us; the launch traced here: 61.5 us
  starting transfers between devices  36.5 us (59%)
  waiting for transfers between devices  15.3 us (25%)
  Pallas kernels  8.38 us (13%)
  between operations  1.37 us (2%)
    all_to_all x1, starting transfers between devices, body(): slab_grads = lax.all_to_all(spread, 'repl', 0, 0, tiled=True)  17.6 us
    ppermute x6, starting transfers between devices, shifted(): return lax.ppermute(array, axis, pairs)  10.2 us
    ppermute x6, waiting for transfers between devices, shifted(): return lax.ppermute(array, axis, pairs)  9.84 us
    all_to_all x1, starting transfers between devices, body(): slab_parts = lax.all_to_all(partial, 'repl', 0, 0, tiled=True)  8.72 us
    all_to_all x1, waiting for transfers between devices, body(): slab_parts = lax.all_to_all(partial, 'repl', 0, 0, tiled=True)  4.43 us
    pallas_call x1, Pallas kernels, body(): pl.pallas_call(late_kernel, out_shape=[pltpu.HBM((blocks, edge, width), j...  2.09 us
    pallas_call x1, Pallas kernels, body(): pl.pallas_call(early_kernel, out_shape=[pltpu.VMEM((slots, edge, edge), j...  1.92 us
    pallas_call x1, Pallas kernels, body(): pl.pallas_call(spread_kernel, out_shape=pltpu.HBM((blocks, width, edge),...  1.79 us
  transfers between devices with their start and end apart: 8, of which 5 were waited for; matrix products, arithmetic and copies ran while one was open for 0% of the time, Pallas kernels for 3%

profile of v2, /device:TPU:1, one launch (start us, length us, event | category | flops | bytes accessed | tf_op | source)
XLA Modules:
  0.0 61.5 jit_solution(6222151632582402920)
XLA Ops:
  0.6 1.8 %spread.1 = bf16[8,128,256]{2,1,0:T(8,128)(2,1)} custom-call(bf16[256,128]{1,0:T(8,128)(2,1)} %grads.1), custom_call_target="tpu_custom_call" | custom-call | tf_op jit(solution)/shard_map/spread/pallas_call | solution.py:233
  2.4 17.6 %all-to-all-start = ((bf16[8,128,256]{2,1,0:T(8,128)(2,1)}), bf16[8,128,256]{2,1,0:T(8,128)(2,1)S(1)}, u32[]{:S(2)}, u32[]{:S(2)}) async-start(bf16[8,128,256]{2,1,0:T(8,128)(2,1)} %spread.1), calls=%async_computation | async-start | bytes 1048576 | tf_op jit(solution)/shard_map/all_to_all | solution.py:247
  20.0 1.3 %collective-permute-start = (bf16[256,128]{1,0:T(8,128)(2,1)}, bf16[256,128]{1,0:T(8,128)(2,1)S(1)}, u32[]{:S(2)}, u32[]{:S(2)}) collective-permute-start(bf16[256,128]{1,0:T(8,128)(2,1)} %features.2), channel_id=1, source_target_pairs={{0,16},{8,24},{16,32},{24,40},{32,48},{40,56},{48,64},{56,72},{64,... | collective-permute-start | bytes 196616 | tf_op jit(solution)/shard_map/ppermute | solution.py:26
  21.3 1.3 %collective-permute-start.1 = (bf16[256,128]{1,0:T(8,128)(2,1)}, bf16[256,128]{1,0:T(8,128)(2,1)S(1)}, u32[]{:S(2)}, u32[]{:S(2)}) collective-permute-start(bf16[256,128]{1,0:T(8,128)(2,1)} %features.2), channel_id=1, source_target_pairs={{16,0},{24,8},{32,16},{40,24},{48,32},{56,40},{64,48},{72,56},{80,... | collective-permute-start | bytes 196616 | tf_op jit(solution)/shard_map/ppermute | solution.py:26
  23.2 0.0 collective-permute-done.below
  23.2 5.2 %collective-permute-done.1.above = bf16[256,128]{1,0:T(8,128)(2,1)S(1)} collective-permute-done((bf16[256,128]{1,0:T(8,128)(2,1)}, bf16[256,128]{1,0:T(8,128)(2,1)S(1)}, u32[]{:S(2)}, u32[]{:S(2)}) %collective-permute-start.1) | collective-permute-done | bytes 65568 | tf_op jit(solution)/shard_map/ppermute | solution.py:26
  28.4 1.0 %all-to-all-done.grads = bf16[8,128,256]{2,1,0:T(8,128)(2,1)S(1)} async-done(((bf16[8,128,256]{2,1,0:T(8,128)(2,1)}), bf16[8,128,256]{2,1,0:T(8,128)(2,1)S(1)}, u32[]{:S(2)}, u32[]{:S(2)}) %all-to-all-start) | async-done | bytes 524320 | tf_op jit(solution)/shard_map/all_to_all | solution.py:247
  29.5 1.9 %early.1 = (bf16[24,256,256]{2,1,0:T(8,128)(2,1)S(1)}, bf16[2,256,128]{2,1,0:T(8,128)(2,1)}, bf16[2,256,128]{2,1,0:T(8,128)(2,1)}, bf16[3,256,128]{2,1,0:T(8,128)(2,1)S(1)}) custom-call(s32[24]{0:T(128)} %bitcast.7, s32[24]{0:T(128)} %bitcast.9, s32[1]{0:T(128)} %bitcast.4.count_from, bf16[24,256,256]{2,1,0:T(8,128)(2,1)} %bitcast.6, ...), custom_call_target="tpu_custom_call" | custom-call | flops 402653184 | bytes 3145728 | tf_op jit(solution)/shard_map/early/pallas_call | solution.py:250
  31.4 0.0 copy-start
  31.4 1.3 %collective-permute-start.2 = (bf16[2,256,128]{2,1,0:T(8,128)(2,1)}, bf16[2,256,128]{2,1,0:T(8,128)(2,1)S(1)}, u32[]{:S(2)}, u32[]{:S(2)}) collective-permute-start(bf16[2,256,128]{2,1,0:T(8,128)(2,1)} %get-tuple-element.14), channel_id=1, source_target_pairs={{0,8},{8,16},{16,24},{24,32},{32,40},{40,48},{48,56},{56,64},{64,7... | collective-permute-start | bytes 393224 | tf_op jit(solution)/shard_map/ppermute | solution.py:26
  32.7 1.3 %collective-permute-start.3 = (bf16[2,256,128]{2,1,0:T(8,128)(2,1)}, bf16[2,256,128]{2,1,0:T(8,128)(2,1)S(1)}, u32[]{:S(2)}, u32[]{:S(2)}) collective-permute-start(bf16[2,256,128]{2,1,0:T(8,128)(2,1)} %get-tuple-element.15), channel_id=1, source_target_pairs={{8,0},{16,8},{24,16},{32,24},{40,32},{48,40},{56,48},{64,56},{72,6... | collective-permute-start | bytes 393224 | tf_op jit(solution)/shard_map/ppermute | solution.py:26
  34.0 0.9 %collective-permute-done.2.from_below = bf16[2,256,128]{2,1,0:T(8,128)(2,1)S(1)} collective-permute-done((bf16[2,256,128]{2,1,0:T(8,128)(2,1)}, bf16[2,256,128]{2,1,0:T(8,128)(2,1)S(1)}, u32[]{:S(2)}, u32[]{:S(2)}) %collective-permute-start.2) | collective-permute-done | bytes 131104 | tf_op jit(solution)/shard_map/ppermute | solution.py:26
  35.0 3.7 %collective-permute-done.3.from_above = bf16[2,256,128]{2,1,0:T(8,128)(2,1)S(1)} collective-permute-done((bf16[2,256,128]{2,1,0:T(8,128)(2,1)}, bf16[2,256,128]{2,1,0:T(8,128)(2,1)S(1)}, u32[]{:S(2)}, u32[]{:S(2)}) %collective-permute-start.3) | collective-permute-done | bytes 131104 | tf_op jit(solution)/shard_map/ppermute | solution.py:26
  38.7 2.1 %late.1 = (bf16[8,256,128]{2,1,0:T(8,128)(2,1)}, bf16[128,256]{1,0:T(8,128)(2,1)}, bf16[128,256]{1,0:T(8,128)(2,1)}, f32[256,128]{1,0:T(8,128)}) custom-call(s32[24]{0:T(128)} %bitcast.8, s32[24]{0:T(128)} %bitcast.10, s32[1]{0:T(128)} %bitcast.5.count_from, bf16[24,256,256]{2,1,0:T(8,128)(2,1)S(1)} %get-tuple-element.12.held, ...), custom_call_target="tpu_custom_call" | custom-call | flops 402653184 | bytes 3145728 | tf_op jit(solution)/shard_map/late/pallas_call | solution.py:275
  40.7 8.7 %all-to-all-start.1 = ((bf16[8,256,128]{2,1,0:T(8,128)(2,1)}), bf16[8,256,128]{2,1,0:T(8,128)(2,1)S(1)}, u32[]{:S(2)}, u32[]{:S(2)}) async-start(bf16[8,256,128]{2,1,0:T(8,128)(2,1)} %get-tuple-element.16), calls=%async_computation.1 | async-start | bytes 1048576 | tf_op jit(solution)/shard_map/all_to_all | solution.py:300
  49.5 3.7 %collective-permute-start.4 = (bf16[128,256]{1,0:T(8,128)(2,1)}, bf16[128,256]{1,0:T(8,128)(2,1)S(1)}, u32[]{:S(2)}, u32[]{:S(2)}) collective-permute-start(bf16[128,256]{1,0:T(8,128)(2,1)} %get-tuple-element.20), channel_id=1, source_target_pairs={{0,16},{8,24},{16,32},{24,40},{32,48},{40,56},{48,64},{56,72},{64,... | collective-permute-start | bytes 196616 | tf_op jit(solution)/shard_map/ppermute | solution.py:26
  53.2 1.3 %collective-permute-start.5 = (bf16[128,256]{1,0:T(8,128)(2,1)}, bf16[128,256]{1,0:T(8,128)(2,1)S(1)}, u32[]{:S(2)}, u32[]{:S(2)}) collective-permute-start(bf16[128,256]{1,0:T(8,128)(2,1)} %get-tuple-element.21), channel_id=1, source_target_pairs={{16,0},{24,8},{32,16},{40,24},{48,32},{56,40},{64,48},{72,56},{80,... | collective-permute-start | bytes 196616 | tf_op jit(solution)/shard_map/ppermute | solution.py:26
  54.5 4.4 %all-to-all-done.1.parts = bf16[8,256,128]{2,1,0:T(8,128)(2,1)S(1)} async-done(((bf16[8,256,128]{2,1,0:T(8,128)(2,1)}), bf16[8,256,128]{2,1,0:T(8,128)(2,1)S(1)}, u32[]{:S(2)}, u32[]{:S(2)}) %all-to-all-start.1) | async-done | bytes 524320 | tf_op jit(solution)/shard_map/all_to_all | solution.py:300
  59.0 0.0 copy-done
  59.0 1.7 %project.1 = (bf16[256,128]{1,0:T(8,128)(2,1)}, f32[256,128]{1,0:T(8,128)S(1)}) custom-call(bf16[8,256,128]{2,1,0:T(8,128)(2,1)S(1)} %all-to-all-done.1.parts, bf16[128,128]{1,0:T(8,128)(2,1)S(1)} %copy-done, f32[256,128]{1,0:T(8,128)} %get-tuple-element.17.kept), custom_call_target="tpu_custom_call" | custom-call | tf_op jit(solution)/shard_map/project/pallas_call | solution.py:303
  60.7 0.0 collective-permute-done.4.from_below
  60.7 0.0 collective-permute-done.5.from_above
  60.7 0.9 %features.3 = bf16[256,128]{1,0:T(8,128)(2,1)} custom-call(f32[256,128]{1,0:T(8,128)S(1)} %get-tuple-element.19.kept, bf16[128,256]{1,0:T(8,128)(2,1)S(1)} %collective-permute-done.4.from_below, bf16[128,256]{1,0:T(8,128)(2,1)S(1)} %collective-permute-done.5.from_above, bf16[128,128]{1,0:T(8,128)(2,1)S(1)} %copy-done), custom_call_target="tpu_custom_call" | custom-call | tf_op jit(solution)/shard_map/features/pallas_call | solution.py:314
Async XLA Ops:
  2.4 27.1 %all-to-all-start = ((bf16[8,128,256]{2,1,0:T(8,128)(2,1)}), bf16[8,128,256]{2,1,0:T(8,128)(2,1)S(1)}, u32[]{:S(2)}, u32[]{:S(2)}) async-start(bf16[8,128,256]{2,1,0:T(8,128)(2,1)} %spread.1), calls=%async_computation | async-start | bytes 1048576 | tf_op jit(solution)/shard_map/all_to_all | solution.py:247
  20.0 3.2 %collective-permute-start = (bf16[256,128]{1,0:T(8,128)(2,1)}, bf16[256,128]{1,0:T(8,128)(2,1)S(1)}, u32[]{:S(2)}, u32[]{:S(2)}) collective-permute-start(bf16[256,128]{1,0:T(8,128)(2,1)} %features.2), channel_id=1, source_target_pairs={{0,16},{8,24},{16,32},{24,40},{32,48},{40,56},{48,64},{56,72},{64,... | collective-permute-start | bytes 196616 | tf_op jit(solution)/shard_map/ppermute | solution.py:26
  21.3 7.2 %collective-permute-start.1 = (bf16[256,128]{1,0:T(8,128)(2,1)}, bf16[256,128]{1,0:T(8,128)(2,1)S(1)}, u32[]{:S(2)}, u32[]{:S(2)}) collective-permute-start(bf16[256,128]{1,0:T(8,128)(2,1)} %features.2), channel_id=1, source_target_pairs={{16,0},{24,8},{32,16},{40,24},{48,32},{56,40},{64,48},{72,56},{80,... | collective-permute-start | bytes 196616 | tf_op jit(solution)/shard_map/ppermute | solution.py:26
  31.4 27.5 %copy-start = (bf16[128,128]{1,0:T(8,128)(2,1)S(1)}, bf16[128,128]{1,0:T(8,128)(2,1)}, u32[]{:S(2)}) copy-start(bf16[128,128]{1,0:T(8,128)(2,1)} %weight.3) | copy-start | bytes 98308
  31.4 3.5 %collective-permute-start.2 = (bf16[2,256,128]{2,1,0:T(8,128)(2,1)}, bf16[2,256,128]{2,1,0:T(8,128)(2,1)S(1)}, u32[]{:S(2)}, u32[]{:S(2)}) collective-permute-start(bf16[2,256,128]{2,1,0:T(8,128)(2,1)} %get-tuple-element.14), channel_id=1, source_target_pairs={{0,8},{8,16},{16,24},{24,32},{32,40},{40,48},{48,56},{56,64},{64,7... | collective-permute-start | bytes 393224 | tf_op jit(solution)/shard_map/ppermute | solution.py:26
  32.7 5.9 %collective-permute-start.3 = (bf16[2,256,128]{2,1,0:T(8,128)(2,1)}, bf16[2,256,128]{2,1,0:T(8,128)(2,1)S(1)}, u32[]{:S(2)}, u32[]{:S(2)}) collective-permute-start(bf16[2,256,128]{2,1,0:T(8,128)(2,1)} %get-tuple-element.15), channel_id=1, source_target_pairs={{8,0},{16,8},{24,16},{32,24},{40,32},{48,40},{56,48},{64,56},{72,6... | collective-permute-start | bytes 393224 | tf_op jit(solution)/shard_map/ppermute | solution.py:26
  40.7 18.2 %all-to-all-start.1 = ((bf16[8,256,128]{2,1,0:T(8,128)(2,1)}), bf16[8,256,128]{2,1,0:T(8,128)(2,1)S(1)}, u32[]{:S(2)}, u32[]{:S(2)}) async-start(bf16[8,256,128]{2,1,0:T(8,128)(2,1)} %get-tuple-element.16), calls=%async_computation.1 | async-start | bytes 1048576 | tf_op jit(solution)/shard_map/all_to_all | solution.py:300
  49.5 11.2 %collective-permute-start.4 = (bf16[128,256]{1,0:T(8,128)(2,1)}, bf16[128,256]{1,0:T(8,128)(2,1)S(1)}, u32[]{:S(2)}, u32[]{:S(2)}) collective-permute-start(bf16[128,256]{1,0:T(8,128)(2,1)} %get-tuple-element.20), channel_id=1, source_target_pairs={{0,16},{8,24},{16,32},{24,40},{32,48},{40,56},{48,64},{56,72},{64,... | collective-permute-start | bytes 196616 | tf_op jit(solution)/shard_map/ppermute | solution.py:26
  53.2 7.5 %collective-permute-start.5 = (bf16[128,256]{1,0:T(8,128)(2,1)}, bf16[128,256]{1,0:T(8,128)(2,1)S(1)}, u32[]{:S(2)}, u32[]{:S(2)}) collective-permute-start(bf16[128,256]{1,0:T(8,128)(2,1)} %get-tuple-element.21), channel_id=1, source_target_pairs={{16,0},{24,8},{32,16},{40,24},{48,32},{56,40},{64,48},{72,56},{80,... | collective-permute-start | bytes 196616 | tf_op jit(solution)/shard_map/ppermute | solution.py:26

commit v3 on v2

v3 whole, which is shorter than its diff:
```python
import jax
import jax.numpy as jnp
from jax import lax
from jax.experimental import pallas as pl
from jax.experimental.pallas import tpu as pltpu
from jax.sharding import PartitionSpec as P

REACH = 2
SPREAD = 2 * REACH + 1
TOGETHER = 4
LIMIT = pltpu.CompilerParams(vmem_limit_bytes=16 * 2**20)

SMEM = pl.BlockSpec(memory_space=pltpu.SMEM)
VMEM = pl.BlockSpec(memory_space=pltpu.VMEM)
ANY = pl.BlockSpec(memory_space=pl.ANY)
HBM = pl.BlockSpec(memory_space=pltpu.HBM)


def in_hbm(array):
    return pltpu.with_memory_space_constraint(array, pltpu.HBM)


def shifted(array, axis, by):
    devices = lax.axis_size(axis)
    pairs = [(i, i + by) for i in range(devices) if 0 <= i + by < devices]
    return lax.ppermute(array, axis, pairs)


def spread_kernel(grads, spread, block, load_sem):
    load = pltpu.make_async_copy(grads, block, load_sem)
    load.start()
    load.wait()
    turned = block[...].T
    for index in range(spread.shape[0]):
        spread[index] = turned


def split_slots(cols, live, lists):
    def place(slot, lengths):
        even, odd = lengths
        is_odd = lax.rem(cols[slot], 2)
        lists[is_odd, jnp.where(is_odd == 1, odd, even)] = slot
        return even + 1 - is_odd, odd + is_odd

    zero = jnp.int32(0)
    return lax.fori_loop(0, live, place, (zero, zero))


def early_kernel(
    rows_from, cols_from, count_from, tiles, features, grads, below, above,
    held, up, down, ends,
    rows, cols, count, lists, back, int_sems, tile_sems, own_sems,
):
    def fetch(slot):
        return pltpu.make_async_copy(tiles.at[slot], held.at[slot], tile_sems.at[slot])

    ints = [
        pltpu.make_async_copy(source, target, int_sems.at[index])
        for index, (source, target) in enumerate(
            ((count_from, count), (rows_from, rows), (cols_from, cols))
        )
    ]
    for copy in ints:
        copy.start()
    own = [
        pltpu.make_async_copy(features, target, own_sems.at[index])
        for index, target in enumerate((ends.at[1], up.at[1], down.at[1]))
    ]
    for copy in own:
        copy.start()
    for slot in range(held.shape[0]):
        fetch(slot).start()
    back[...] = jnp.zeros_like(back)
    ends[0] = below[...]
    ends[2] = above[...]
    for copy in ints:
        copy.wait()
    even, odd = split_slots(cols, count[0], lists)

    @pl.loop(0, lax.div(odd + TOGETHER - 1, TOGETHER))
    def _(step):
        sums = []
        slots = []
        for k in range(TOGETHER):
            place = step * TOGETHER + k
            slot = lists[1, jnp.minimum(place, odd - 1)]
            slots.append((place < odd, slot))

            @pl.when(place < odd)
            def _():
                fetch(slot).wait()

        for used, slot in slots:
            term = jnp.dot(grads[rows[slot]], held[slot], preferred_element_type=jnp.float32)
            sums.append((jnp.where(used, lax.div(cols[slot], 2), 2), term))
        for index, term in sums:
            back[index] += term

    for index, target in enumerate((down, up)):
        target[0] = back[index].T.astype(target.dtype)

    @pl.loop(0, even)
    def _(place):
        fetch(lists[0, place]).wait()

    @pl.loop(count[0], held.shape[0])
    def _(slot):
        fetch(slot).wait()

    for copy in own:
        copy.wait()


def load_ints(rows_from, cols_from, count_from, rows, cols, count, sems):
    copies = [
        pltpu.make_async_copy(source, target, sems.at[index])
        for index, (source, target) in enumerate(
            ((count_from, count), (rows_from, rows), (cols_from, cols))
        )
    ]
    for copy in copies:
        copy.start()
    return copies


def middle_kernel(
    rows_from, cols_from, count_from, held, grads, ends,
    sums, far_down, center, far_up,
    rows, cols, count, lists, total, back, int_sems,
):
    blocks = grads.shape[0]
    ints = load_ints(rows_from, cols_from, count_from, rows, cols, count, int_sems)
    total[...] = jnp.zeros_like(total)
    back[...] = jnp.zeros_like(back)
    for copy in ints:
        copy.wait()
    even, _ = split_slots(cols, count[0], lists)

    @pl.loop(0, lax.div(even + TOGETHER - 1, TOGETHER))
    def _(step):
        terms = []
        for k in range(TOGETHER):
            place = step * TOGETHER + k
            slot = lists[0, jnp.minimum(place, even - 1)]
            used = place < even
            row, side = rows[slot], lax.div(cols[slot], 2)
            tile = held[slot]
            ahead = jnp.dot(tile, ends[side], preferred_element_type=jnp.float32)
            behind = jnp.dot(grads[row], tile, preferred_element_type=jnp.float32)
            terms.append((total, jnp.where(used, row, blocks), ahead))
            terms.append((back, jnp.where(used, side, 3), behind))
        for target, index, term in terms:
            target[index] += term

    sums[...] = total[pl.ds(0, blocks)]
    for side, ref in enumerate((far_down, center, far_up)):
        ref[...] = back[side].astype(ref.dtype)


def late_kernel(
    rows_from, cols_from, count_from, held, sums, center, from_below, from_above,
    parts, kept,
    rows, cols, count, lists, near, total, int_sems,
):
    blocks = sums.shape[0]
    ints = load_ints(rows_from, cols_from, count_from, rows, cols, count, int_sems)
    near[0] = from_below[1]
    near[1] = from_above[1]
    total[pl.ds(0, blocks)] = sums[...]
    for copy in ints:
        copy.wait()
    _, odd = split_slots(cols, count[0], lists)

    @pl.loop(0, lax.div(odd + TOGETHER - 1, TOGETHER))
    def _(step):
        terms = []
        for k in range(TOGETHER):
            place = step * TOGETHER + k
            slot = lists[1, jnp.minimum(place, odd - 1)]
            ahead = jnp.dot(
                held[slot], near[lax.div(cols[slot], 2)], preferred_element_type=jnp.float32
            )
            terms.append((jnp.where(place < odd, rows[slot], blocks), ahead))
        for index, term in terms:
            total[index] += term

    parts[...] = total[pl.ds(0, blocks)].astype(parts.dtype)
    kept[...] = (
        center[...].T + from_below[0].astype(jnp.float32) + from_above[0].astype(jnp.float32)
    )


def project_kernel(parts, weight, kept, out, kept_out):
    total = jnp.sum(parts[...].astype(jnp.float32), axis=0)
    out[...] = jnp.dot(
        total.astype(jnp.bfloat16), weight[...], preferred_element_type=jnp.float32
    ).astype(out.dtype)
    kept_out[...] = kept[...]


def features_kernel(kept, from_below, from_above, weight, out):
    far = from_below[...].astype(jnp.float32) + from_above[...].astype(jnp.float32)
    total = kept[...] + far.T
    out[...] = lax.dot_general(
        total.astype(jnp.bfloat16),
        weight[...],
        (((1,), (1,)), ((), ())),
        preferred_element_type=jnp.float32,
    ).astype(out.dtype)


def body(features, weight, grad_out, tile_values, tile_rows, tile_cols, tile_count):
    slots, edge = tile_values.shape[2], tile_values.shape[3]
    width = features.shape[1]
    blocks = lax.axis_size("repl")
    tiles = in_hbm(tile_values.reshape(slots, edge, edge))
    ints = [
        in_hbm(tile_rows.reshape(slots)),
        in_hbm(tile_cols.reshape(slots)),
        tile_count.reshape(1),
    ]
    int_scratch = [
        pltpu.SMEM((slots,), jnp.int32),
        pltpu.SMEM((slots,), jnp.int32),
        pltpu.SMEM((1,), jnp.int32),
        pltpu.SMEM((2, slots), jnp.int32),
    ]
    flops = 2 * slots * edge * edge * width
    moved = slots * edge * edge * 2

    spread = pl.pallas_call(
        spread_kernel,
        out_shape=pltpu.VMEM((blocks, width, edge), jnp.bfloat16),
        in_specs=[HBM],
        out_specs=VMEM,
        scratch_shapes=[
            pltpu.VMEM((edge, width), jnp.bfloat16),
            pltpu.SemaphoreType.DMA,
        ],
        compiler_params=LIMIT,
        name="spread",
    )(in_hbm(grad_out))
    slab_grads = lax.all_to_all(spread, "repl", 0, 0, tiled=True)
    below = shifted(features, "dom", REACH)
    above = shifted(features, "dom", -REACH)
    held, up, down, ends = pl.pallas_call(
        early_kernel,
        out_shape=[
            pltpu.VMEM((slots, edge, edge), jnp.bfloat16),
            pltpu.VMEM((2, edge, width), jnp.bfloat16),
            pltpu.VMEM((2, edge, width), jnp.bfloat16),
            pltpu.VMEM((3, edge, width), jnp.bfloat16),
        ],
        in_specs=[HBM] * 2 + [ANY] + [HBM] * 2 + [VMEM] * 3,
        out_specs=[VMEM] * 4,
        scratch_shapes=int_scratch
        + [
            pltpu.VMEM((3, width, edge), jnp.float32),
            pltpu.SemaphoreType.DMA((3,)),
            pltpu.SemaphoreType.DMA((slots,)),
            pltpu.SemaphoreType.DMA((3,)),
        ],
        cost_estimate=pl.CostEstimate(flops=flops, bytes_accessed=moved, transcendentals=0),
        compiler_params=LIMIT,
        name="early",
    )(*ints, tiles, in_hbm(features), slab_grads, below, above)
    from_below = shifted(up, "dom", 1)
    from_above = shifted(down, "dom", -1)
    cost = pl.CostEstimate(flops=flops, bytes_accessed=moved, transcendentals=0)
    term = pltpu.VMEM((width, edge), jnp.bfloat16)
    sums, far_down, center, far_up = pl.pallas_call(
        middle_kernel,
        out_shape=[
            pltpu.VMEM((blocks, edge, width), jnp.float32),
            term,
            pltpu.VMEM((width, edge), jnp.float32),
            term,
        ],
        in_specs=[HBM] * 2 + [ANY] + [VMEM] * 3,
        out_specs=[VMEM] * 4,
        scratch_shapes=int_scratch
        + [
            pltpu.VMEM((blocks + 1, edge, width), jnp.float32),
            pltpu.VMEM((4, width, edge), jnp.float32),
            pltpu.SemaphoreType.DMA((3,)),
        ],
        cost_estimate=cost,
        compiler_params=LIMIT,
        name="middle",
    )(*ints, held, slab_grads, ends)
    partial, kept = pl.pallas_call(
        late_kernel,
        out_shape=[
            pltpu.VMEM((blocks, edge, width), jnp.bfloat16),
            pltpu.VMEM((edge, width), jnp.float32),
        ],
        in_specs=[HBM] * 2 + [ANY] + [VMEM] * 5,
        out_specs=[VMEM] * 2,
        scratch_shapes=int_scratch
        + [
            pltpu.VMEM((2, edge, width), jnp.bfloat16),
            pltpu.VMEM((blocks + 1, edge, width), jnp.float32),
            pltpu.SemaphoreType.DMA((3,)),
        ],
        cost_estimate=cost,
        compiler_params=LIMIT,
        name="late",
    )(*ints, held, sums, center, from_below, from_above)
    slab_parts = lax.all_to_all(partial, "repl", 0, 0, tiled=True)
    far_from_above = shifted(far_down, "dom", -REACH)
    far_from_below = shifted(far_up, "dom", REACH)
    block = jax.ShapeDtypeStruct((edge, width), jnp.bfloat16)
    projected, kept = pl.pallas_call(
        project_kernel,
        out_shape=[block, pltpu.VMEM((edge, width), jnp.float32)],
        in_specs=[VMEM] * 3,
        out_specs=[VMEM] * 2,
        compiler_params=LIMIT,
        name="project",
    )(slab_parts, weight, kept)
    grad_features = pl.pallas_call(
        features_kernel,
        out_shape=block,
        in_specs=[VMEM] * 4,
        out_specs=VMEM,
        compiler_params=LIMIT,
        name="features",
    )(kept, far_from_below, far_from_above, weight)
    return projected, grad_features


def solution(mesh):
    placed = (
        P(("dom", "repl"), None),
        P(),
        P(("dom", "repl"), None),
        P("dom", "repl", None, None, None),
        P("dom", "repl", None),
        P("dom", "repl", None),
        P("dom", "repl"),
    )
    return jax.shard_map(
        body,
        mesh=mesh,
        in_specs=placed,
        out_specs=(P(("dom", "repl"), None), P(("dom", "repl"), None)),
        check_vma=False,
    )
```

time: 62.2 us -> 58.4 us (0.939)
  starting transfers between devices: 36.5 us -> 31.4 us
    all_to_all x1, starting transfers between devices: 8.72 us -> 5.28 us  [body(): slab_parts = lax.all_to_all(partial, 'repl', 0, 0, tiled=True)]
    all_to_all x1, waiting for transfers between devices: 4.43 us -> 6.12 us  [body(): slab_parts = lax.all_to_all(partial, 'repl', 0, 0, tiled=True)]
    ppermute x6, starting transfers between devices: 10.2 us -> 8.51 us  [shifted(): return lax.ppermute(array, axis, pairs)]
    ppermute x6, waiting for transfers between devices: 9.84 us -> 8.55 us  [shifted(): return lax.ppermute(array, axis, pairs)]
    pallas_call x4 -> x5, Pallas kernels: 6.46 us -> 6.75 us  [the longest x1 1.97 us: body(): pl.pallas_call(late_kernel, out_shape=[pltpu.VMEM((blocks, edge, width),...]
  transfers between devices with their start and end apart: 8 -> 8, of which waited for: 5 -> 4; matrix products, arithmetic and copies ran while one was open for 0% -> 0% of each run, Pallas kernels for 3% -> 4%
where the time goes in v3:
time: 58.4 us; the launch traced here: 57.4 us
  starting transfers between devices  31.4 us (54%)
  waiting for transfers between devices  15.7 us (27%)
  Pallas kernels  8.99 us (15%)
  between operations  1.38 us (2%)
    all_to_all x1, starting transfers between devices, body(): slab_grads = lax.all_to_all(spread, 'repl', 0, 0, tiled=True)  17.6 us
    ppermute x6, waiting for transfers between devices, shifted(): return lax.ppermute(array, axis, pairs)  8.55 us
    ppermute x6, starting transfers between devices, shifted(): return lax.ppermute(array, axis, pairs)  8.51 us
    all_to_all x1, waiting for transfers between devices, body(): slab_parts = lax.all_to_all(partial, 'repl', 0, 0, tiled=True)  6.12 us
    all_to_all x1, starting transfers between devices, body(): slab_parts = lax.all_to_all(partial, 'repl', 0, 0, tiled=True)  5.28 us
    pallas_call x1, Pallas kernels, body(): pl.pallas_call(early_kernel, out_shape=[pltpu.VMEM((slots, edge, edge), j...  2.24 us
    pallas_call x1, Pallas kernels, body(): pl.pallas_call(late_kernel, out_shape=[pltpu.VMEM((blocks, edge, width),...  1.97 us
    pallas_call x1, Pallas kernels, body(): pl.pallas_call(spread_kernel, out_shape=pltpu.VMEM((blocks, width, edge),...  1.73 us
  transfers between devices with their start and end apart: 8, of which 4 were waited for; matrix products, arithmetic and copies ran while one was open for 0% of the time, Pallas kernels for 4%

profile of v3, /device:TPU:1, one launch (start us, length us, event | category | flops | bytes accessed | tf_op | source)
XLA Modules:
  0.0 57.4 jit_solution(3853863317018944976)
XLA Ops:
  0.6 1.7 %spread.1 = bf16[8,128,256]{2,1,0:T(8,128)(2,1)} custom-call(bf16[256,128]{1,0:T(8,128)(2,1)} %grads.1), custom_call_target="tpu_custom_call" | custom-call | tf_op jit(solution)/shard_map/spread/pallas_call | solution.py:231
  2.4 17.6 %all-to-all-start = ((bf16[8,128,256]{2,1,0:T(8,128)(2,1)}), bf16[8,128,256]{2,1,0:T(8,128)(2,1)S(1)}, u32[]{:S(2)}, u32[]{:S(2)}) async-start(bf16[8,128,256]{2,1,0:T(8,128)(2,1)} %spread.1), calls=%async_computation | async-start | bytes 1048576 | tf_op jit(solution)/shard_map/all_to_all | solution.py:243
  19.9 1.3 %collective-permute-start = (bf16[256,128]{1,0:T(8,128)(2,1)}, bf16[256,128]{1,0:T(8,128)(2,1)S(1)}, u32[]{:S(2)}, u32[]{:S(2)}) collective-permute-start(bf16[256,128]{1,0:T(8,128)(2,1)} %features.2), channel_id=1, source_target_pairs={{0,16},{8,24},{16,32},{24,40},{32,48},{40,56},{48,64},{56,72},{64,... | collective-permute-start | bytes 196616 | tf_op jit(solution)/shard_map/ppermute | solution.py:26
  21.2 1.3 %collective-permute-start.1 = (bf16[256,128]{1,0:T(8,128)(2,1)}, bf16[256,128]{1,0:T(8,128)(2,1)S(1)}, u32[]{:S(2)}, u32[]{:S(2)}) collective-permute-start(bf16[256,128]{1,0:T(8,128)(2,1)} %features.2), channel_id=1, source_target_pairs={{16,0},{24,8},{32,16},{40,24},{48,32},{56,40},{64,48},{72,56},{80,... | collective-permute-start | bytes 196616 | tf_op jit(solution)/shard_map/ppermute | solution.py:26
  23.2 0.0 collective-permute-done.below
  23.2 5.2 %collective-permute-done.1.above = bf16[256,128]{1,0:T(8,128)(2,1)S(1)} collective-permute-done((bf16[256,128]{1,0:T(8,128)(2,1)}, bf16[256,128]{1,0:T(8,128)(2,1)S(1)}, u32[]{:S(2)}, u32[]{:S(2)}) %collective-permute-start.1) | collective-permute-done | bytes 65568 | tf_op jit(solution)/shard_map/ppermute | solution.py:26
  28.4 1.0 %all-to-all-done.grads = bf16[8,128,256]{2,1,0:T(8,128)(2,1)S(1)} async-done(((bf16[8,128,256]{2,1,0:T(8,128)(2,1)}), bf16[8,128,256]{2,1,0:T(8,128)(2,1)S(1)}, u32[]{:S(2)}, u32[]{:S(2)}) %all-to-all-start) | async-done | bytes 524320 | tf_op jit(solution)/shard_map/all_to_all | solution.py:243
  29.4 2.2 %early.1 = (bf16[24,256,256]{2,1,0:T(8,128)(2,1)S(1)}, bf16[2,256,128]{2,1,0:T(8,128)(2,1)S(1)}, bf16[2,256,128]{2,1,0:T(8,128)(2,1)S(1)}, bf16[3,256,128]{2,1,0:T(8,128)(2,1)S(1)}) custom-call(s32[24]{0:T(128)} %bitcast.8, s32[24]{0:T(128)} %bitcast.11, s32[1]{0:T(128)} %bitcast.4.count_from, bf16[24,256,256]{2,1,0:T(8,128)(2,1)} %bitcast.7, ...), custom_call_target="tpu_custom_call" | custom-call | flops 402653184 | bytes 3145728 | tf_op jit(solution)/shard_map/early/pallas_call | solution.py:246
  31.7 1.3 %collective-permute-start.2 = (bf16[2,256,128]{2,1,0:T(8,128)(2,1)S(1)}, bf16[2,256,128]{2,1,0:T(8,128)(2,1)S(1)}, u32[]{:S(2)}, u32[]{:S(2)}) collective-permute-start(bf16[2,256,128]{2,1,0:T(8,128)(2,1)S(1)} %get-tuple-element.18), channel_id=1, source_target_pairs={{0,8},{8,16},{16,24},{24,32},{32,40},{40,48},{48,56},{56,64},{64,7... | collective-permute-start | bytes 393224 | tf_op jit(solution)/shard_map/ppermute | solution.py:26
  33.0 1.3 %collective-permute-start.3 = (bf16[2,256,128]{2,1,0:T(8,128)(2,1)S(1)}, bf16[2,256,128]{2,1,0:T(8,128)(2,1)S(1)}, u32[]{:S(2)}, u32[]{:S(2)}) collective-permute-start(bf16[2,256,128]{2,1,0:T(8,128)(2,1)S(1)} %get-tuple-element.19), channel_id=1, source_target_pairs={{8,0},{16,8},{24,16},{32,24},{40,32},{48,40},{56,48},{64,56},{72,6... | collective-permute-start | bytes 393224 | tf_op jit(solution)/shard_map/ppermute | solution.py:26
  34.3 1.4 %middle.1 = (f32[8,256,128]{2,1,0:T(8,128)S(1)}, bf16[128,256]{1,0:T(8,128)(2,1)S(1)}, f32[128,256]{1,0:T(8,128)S(1)}, bf16[128,256]{1,0:T(8,128)(2,1)S(1)}) custom-call(s32[24]{0:T(128)} %bitcast.9, s32[24]{0:T(128)} %bitcast.12, s32[1]{0:T(128)} %bitcast.5.count_from, bf16[24,256,256]{2,1,0:T(8,128)(2,1)S(1)} %get-tuple-element.14.held, ...), custom_call_target="tpu_custom_call" | custom-call | flops 402653184 | bytes 3145728 | tf_op jit(solution)/shard_map/middle/pallas_call | solution.py:271
  35.7 0.0 copy-start
  35.7 0.0 collective-permute-done.2.from_below
  35.7 3.3 %collective-permute-done.3.from_above = bf16[2,256,128]{2,1,0:T(8,128)(2,1)S(1)} collective-permute-done((bf16[2,256,128]{2,1,0:T(8,128)(2,1)S(1)}, bf16[2,256,128]{2,1,0:T(8,128)(2,1)S(1)}, u32[]{:S(2)}, u32[]{:S(2)}) %collective-permute-start.3) | collective-permute-done | bytes 131104 | tf_op jit(solution)/shard_map/ppermute | solution.py:26
  39.0 2.0 %late.1 = (bf16[8,256,128]{2,1,0:T(8,128)(2,1)}, f32[256,128]{1,0:T(8,128)S(1)}) custom-call(s32[24]{0:T(128)} %bitcast.10, s32[24]{0:T(128)} %bitcast.13, s32[1]{0:T(128)} %bitcast.6.count_from, bf16[24,256,256]{2,1,0:T(8,128)(2,1)S(1)} %get-tuple-element.14.held, f32[8,256,128]{2,1,0:T(8,128)S(1)} %get-tuple-element.16.sums, ...), custom_call_target="tpu_custom_call" | custom-call | flops 402653184 | bytes 3145728 | tf_op jit(solution)/shard_map/late/pallas_call | solution.py:291
  41.0 5.3 %all-to-all-start.1 = ((bf16[8,256,128]{2,1,0:T(8,128)(2,1)}), bf16[8,256,128]{2,1,0:T(8,128)(2,1)S(1)}, u32[]{:S(2)}, u32[]{:S(2)}) async-start(bf16[8,256,128]{2,1,0:T(8,128)(2,1)} %get-tuple-element.20), calls=%async_computation.1 | async-start | bytes 1048576 | tf_op jit(solution)/shard_map/all_to_all | solution.py:309
  46.3 2.1 %collective-permute-start.4 = (bf16[128,256]{1,0:T(8,128)(2,1)S(1)}, bf16[128,256]{1,0:T(8,128)(2,1)S(1)}, u32[]{:S(2)}, u32[]{:S(2)}) collective-permute-start(bf16[128,256]{1,0:T(8,128)(2,1)S(1)} %get-tuple-element.24), channel_id=1, source_target_pairs={{0,16},{8,24},{16,32},{24,40},{32,48},{40,56},{48,64},{56,72},{64,... | collective-permute-start | bytes 196616 | tf_op jit(solution)/shard_map/ppermute | solution.py:26
  48.3 1.3 %collective-permute-start.5 = (bf16[128,256]{1,0:T(8,128)(2,1)S(1)}, bf16[128,256]{1,0:T(8,128)(2,1)S(1)}, u32[]{:S(2)}, u32[]{:S(2)}) collective-permute-start(bf16[128,256]{1,0:T(8,128)(2,1)S(1)} %get-tuple-element.25), channel_id=1, source_target_pairs={{16,0},{24,8},{32,16},{40,24},{48,32},{56,40},{64,48},{72,56},{80,... | collective-permute-start | bytes 196616 | tf_op jit(solution)/shard_map/ppermute | solution.py:26
  49.6 6.1 %all-to-all-done.1.parts = bf16[8,256,128]{2,1,0:T(8,128)(2,1)S(1)} async-done(((bf16[8,256,128]{2,1,0:T(8,128)(2,1)}), bf16[8,256,128]{2,1,0:T(8,128)(2,1)S(1)}, u32[]{:S(2)}, u32[]{:S(2)}) %all-to-all-start.1) | async-done | bytes 524320 | tf_op jit(solution)/shard_map/all_to_all | solution.py:309
  55.8 0.0 copy-done
  55.8 0.8 %project.1 = (bf16[256,128]{1,0:T(8,128)(2,1)}, f32[256,128]{1,0:T(8,128)S(1)}) custom-call(bf16[8,256,128]{2,1,0:T(8,128)(2,1)S(1)} %all-to-all-done.1.parts, bf16[128,128]{1,0:T(8,128)(2,1)S(1)} %copy-done, f32[256,128]{1,0:T(8,128)S(1)} %get-tuple-element.21.kept), custom_call_target="tpu_custom_call" | custom-call | tf_op jit(solution)/shard_map/project/pallas_call | solution.py:313
  56.6 0.0 collective-permute-done.4.from_below
  56.6 0.0 collective-permute-done.5.from_above
  56.6 0.9 %features.3 = bf16[256,128]{1,0:T(8,128)(2,1)} custom-call(f32[256,128]{1,0:T(8,128)S(1)} %get-tuple-element.23.kept, bf16[128,256]{1,0:T(8,128)(2,1)S(1)} %collective-permute-done.4.from_below, bf16[128,256]{1,0:T(8,128)(2,1)S(1)} %collective-permute-done.5.from_above, bf16[128,128]{1,0:T(8,128)(2,1)S(1)} %copy-done), custom_call_target="tpu_custom_call" | custom-call | tf_op jit(solution)/shard_map/features/pallas_call | solution.py:321
Async XLA Ops:
  2.4 27.1 %all-to-all-start = ((bf16[8,128,256]{2,1,0:T(8,128)(2,1)}), bf16[8,128,256]{2,1,0:T(8,128)(2,1)S(1)}, u32[]{:S(2)}, u32[]{:S(2)}) async-start(bf16[8,128,256]{2,1,0:T(8,128)(2,1)} %spread.1), calls=%async_computation | async-start | bytes 1048576 | tf_op jit(solution)/shard_map/all_to_all | solution.py:243
  19.9 3.2 %collective-permute-start = (bf16[256,128]{1,0:T(8,128)(2,1)}, bf16[256,128]{1,0:T(8,128)(2,1)S(1)}, u32[]{:S(2)}, u32[]{:S(2)}) collective-permute-start(bf16[256,128]{1,0:T(8,128)(2,1)} %features.2), channel_id=1, source_target_pairs={{0,16},{8,24},{16,32},{24,40},{32,48},{40,56},{48,64},{56,72},{64,... | collective-permute-start | bytes 196616 | tf_op jit(solution)/shard_map/ppermute | solution.py:26
  21.2 7.2 %collective-permute-start.1 = (bf16[256,128]{1,0:T(8,128)(2,1)}, bf16[256,128]{1,0:T(8,128)(2,1)S(1)}, u32[]{:S(2)}, u32[]{:S(2)}) collective-permute-start(bf16[256,128]{1,0:T(8,128)(2,1)} %features.2), channel_id=1, source_target_pairs={{16,0},{24,8},{32,16},{40,24},{48,32},{56,40},{64,48},{72,56},{80,... | collective-permute-start | bytes 196616 | tf_op jit(solution)/shard_map/ppermute | solution.py:26
  31.7 4.0 %collective-permute-start.2 = (bf16[2,256,128]{2,1,0:T(8,128)(2,1)S(1)}, bf16[2,256,128]{2,1,0:T(8,128)(2,1)S(1)}, u32[]{:S(2)}, u32[]{:S(2)}) collective-permute-start(bf16[2,256,128]{2,1,0:T(8,128)(2,1)S(1)} %get-tuple-element.18), channel_id=1, source_target_pairs={{0,8},{8,16},{16,24},{24,32},{32,40},{40,48},{48,56},{56,64},{64,7... | collective-permute-start | bytes 393224 | tf_op jit(solution)/shard_map/ppermute | solution.py:26
  33.0 6.0 %collective-permute-start.3 = (bf16[2,256,128]{2,1,0:T(8,128)(2,1)S(1)}, bf16[2,256,128]{2,1,0:T(8,128)(2,1)S(1)}, u32[]{:S(2)}, u32[]{:S(2)}) collective-permute-start(bf16[2,256,128]{2,1,0:T(8,128)(2,1)S(1)} %get-tuple-element.19), channel_id=1, source_target_pairs={{8,0},{16,8},{24,16},{32,24},{40,32},{48,40},{56,48},{64,56},{72,6... | collective-permute-start | bytes 393224 | tf_op jit(solution)/shard_map/ppermute | solution.py:26
  35.7 20.1 %copy-start = (bf16[128,128]{1,0:T(8,128)(2,1)S(1)}, bf16[128,128]{1,0:T(8,128)(2,1)}, u32[]{:S(2)}) copy-start(bf16[128,128]{1,0:T(8,128)(2,1)} %weight.3) | copy-start | bytes 98308
  41.0 14.8 %all-to-all-start.1 = ((bf16[8,256,128]{2,1,0:T(8,128)(2,1)}), bf16[8,256,128]{2,1,0:T(8,128)(2,1)S(1)}, u32[]{:S(2)}, u32[]{:S(2)}) async-start(bf16[8,256,128]{2,1,0:T(8,128)(2,1)} %get-tuple-element.20), calls=%async_computation.1 | async-start | bytes 1048576 | tf_op jit(solution)/shard_map/all_to_all | solution.py:309
  46.3 10.3 %collective-permute-start.4 = (bf16[128,256]{1,0:T(8,128)(2,1)S(1)}, bf16[128,256]{1,0:T(8,128)(2,1)S(1)}, u32[]{:S(2)}, u32[]{:S(2)}) collective-permute-start(bf16[128,256]{1,0:T(8,128)(2,1)S(1)} %get-tuple-element.24), channel_id=1, source_target_pairs={{0,16},{8,24},{16,32},{24,40},{32,48},{40,56},{48,64},{56,72},{64,... | collective-permute-start | bytes 196616 | tf_op jit(solution)/shard_map/ppermute | solution.py:26
  48.3 8.2 %collective-permute-start.5 = (bf16[128,256]{1,0:T(8,128)(2,1)S(1)}, bf16[128,256]{1,0:T(8,128)(2,1)S(1)}, u32[]{:S(2)}, u32[]{:S(2)}) collective-permute-start(bf16[128,256]{1,0:T(8,128)(2,1)S(1)} %get-tuple-element.25), channel_id=1, source_target_pairs={{16,0},{24,8},{32,16},{40,24},{48,32},{56,40},{64,48},{72,56},{80,... | collective-permute-start | bytes 196616 | tf_op jit(solution)/shard_map/ppermute | solution.py:26

commit v4 on v3

v4 whole, which is shorter than its diff:
```python
import jax
import jax.numpy as jnp
from jax import lax
from jax.experimental import pallas as pl
from jax.experimental.pallas import tpu as pltpu
from jax.sharding import PartitionSpec as P

REACH = 2
SPREAD = 2 * REACH + 1
TOGETHER = 4
KEPT = 22
LIMIT = pltpu.CompilerParams(vmem_limit_bytes=16 * 2**20)

SMEM = pl.BlockSpec(memory_space=pltpu.SMEM)
VMEM = pl.BlockSpec(memory_space=pltpu.VMEM)
ANY = pl.BlockSpec(memory_space=pl.ANY)
HBM = pl.BlockSpec(memory_space=pltpu.HBM)


def in_hbm(array):
    return pltpu.with_memory_space_constraint(array, pltpu.HBM)


def shifted(array, axis, by):
    devices = lax.axis_size(axis)
    pairs = [(i, i + by) for i in range(devices) if 0 <= i + by < devices]
    return lax.ppermute(array, axis, pairs)


def spread_kernel(
    grads, rows_from, cols_from, spread, rows, cols, block, sems
):
    loads = [
        pltpu.make_async_copy(source, target, sems.at[index])
        for index, (source, target) in enumerate(
            ((grads, block), (rows_from, rows), (cols_from, cols))
        )
    ]
    for load in loads:
        load.start()
    loads[0].wait()
    turned = block[...].T
    for index in range(spread.shape[0]):
        spread[index] = turned
    for load in loads[1:]:
        load.wait()


def split_slots(cols, live, lists):
    def place(slot, lengths):
        even, odd = lengths
        is_odd = lax.rem(cols[slot], 2)
        lists[is_odd, jnp.where(is_odd == 1, odd, even)] = slot
        return even + 1 - is_odd, odd + is_odd

    zero = jnp.int32(0)
    return lax.fori_loop(0, live, place, (zero, zero))


def hold_kernel(cols, count, tiles, held, lists, sems):
    _, odd = split_slots(cols, count[0, 0], lists)

    def fetch(place):
        return pltpu.make_async_copy(tiles.at[lists[1, place]], held.at[place], sems.at[place])

    @pl.loop(0, jnp.minimum(odd, KEPT))
    def _(place):
        fetch(place).start()

    @pl.loop(0, jnp.minimum(odd, KEPT))
    def _(place):
        fetch(place).wait()


def over_odd_tiles(lists, odd, tiles, held, extra, extra_sem, product, add):
    ready = jnp.minimum(odd, KEPT)

    @pl.loop(0, lax.div(ready + TOGETHER - 1, TOGETHER))
    def _(step):
        terms = []
        for k in range(TOGETHER):
            place = step * TOGETHER + k
            inside = jnp.minimum(place, ready - 1)
            slot = lists[1, inside]
            terms.append((slot, place < ready, product(slot, held[inside])))
        for slot, used, term in terms:
            add(slot, used, term)

    @pl.loop(ready, odd)
    def _(place):
        slot = lists[1, place]
        copy = pltpu.make_async_copy(tiles.at[slot], extra, extra_sem)
        copy.start()
        copy.wait()
        add(slot, True, product(slot, extra[...]))


def early_kernel(
    rows, cols, count, tiles, features, held, grads, below, above,
    up, down, ends,
    lists, back, extra, extra_sem, own_sems,
):
    own = [
        pltpu.make_async_copy(features, target, own_sems.at[index])
        for index, target in enumerate((ends.at[1], up.at[1], down.at[1]))
    ]
    for copy in own:
        copy.start()
    back[...] = jnp.zeros_like(back)
    ends[0] = below[...]
    ends[2] = above[...]
    _, odd = split_slots(cols, count[0, 0], lists)

    def product(slot, tile):
        return jnp.dot(grads[rows[slot]], tile, preferred_element_type=jnp.float32)

    def add(slot, used, term):
        back[jnp.where(used, lax.div(cols[slot], 2), 2)] += term

    over_odd_tiles(lists, odd, tiles, held, extra, extra_sem, product, add)
    for index, target in enumerate((down, up)):
        target[0] = back[index].T.astype(target.dtype)
    for copy in own:
        copy.wait()


def middle_kernel(
    rows, cols, count, tiles, grads, ends,
    sums, far_down, center, far_up,
    lists, held, total, back, sems,
):
    blocks = grads.shape[0]
    even, _ = split_slots(cols, count[0, 0], lists)

    def fetch(place):
        return pltpu.make_async_copy(tiles.at[lists[0, place]], held.at[place], sems.at[place])

    @pl.loop(0, even)
    def _(place):
        fetch(place).start()

    total[...] = jnp.zeros_like(total)
    back[...] = jnp.zeros_like(back)

    @pl.loop(0, lax.div(even + TOGETHER - 1, TOGETHER))
    def _(step):
        terms = []
        for k in range(TOGETHER):
            place = step * TOGETHER + k

            @pl.when(place < even)
            def _():
                fetch(place).wait()

        for k in range(TOGETHER):
            place = step * TOGETHER + k
            inside = jnp.minimum(place, even - 1)
            slot = lists[0, inside]
            used = place < even
            row, side = rows[slot], lax.div(cols[slot], 2)
            tile = held[inside]
            ahead = jnp.dot(tile, ends[side], preferred_element_type=jnp.float32)
            behind = jnp.dot(grads[row], tile, preferred_element_type=jnp.float32)
            terms.append((total, jnp.where(used, row, blocks), ahead))
            terms.append((back, jnp.where(used, side, 3), behind))
        for target, index, term in terms:
            target[index] += term

    sums[...] = total[pl.ds(0, blocks)]
    for side, ref in enumerate((far_down, center, far_up)):
        ref[...] = back[side].astype(ref.dtype)


def late_kernel(
    rows, cols, count, tiles, held, sums, center, from_above, from_below,
    parts, kept,
    lists, near, total, extra, extra_sem,
):
    blocks = sums.shape[0]
    near[0] = from_below[1]
    near[1] = from_above[1]
    total[pl.ds(0, blocks)] = sums[...]
    _, odd = split_slots(cols, count[0, 0], lists)

    def product(slot, tile):
        block = near[lax.div(cols[slot], 2)]
        return jnp.dot(tile, block, preferred_element_type=jnp.float32)

    def add(slot, used, term):
        total[jnp.where(used, rows[slot], blocks)] += term

    over_odd_tiles(lists, odd, tiles, held, extra, extra_sem, product, add)
    parts[...] = total[pl.ds(0, blocks)].astype(parts.dtype)
    kept[...] = (
        center[...].T + from_below[0].astype(jnp.float32) + from_above[0].astype(jnp.float32)
    )


def project_kernel(parts, weight, kept, out, kept_out):
    total = jnp.sum(parts[...].astype(jnp.float32), axis=0)
    out[...] = jnp.dot(
        total.astype(jnp.bfloat16), weight[...], preferred_element_type=jnp.float32
    ).astype(out.dtype)
    kept_out[...] = kept[...]


def features_kernel(kept, from_below, from_above, weight, out):
    far = from_below[...].astype(jnp.float32) + from_above[...].astype(jnp.float32)
    total = kept[...] + far.T
    out[...] = lax.dot_general(
        total.astype(jnp.bfloat16),
        weight[...],
        (((1,), (1,)), ((), ())),
        preferred_element_type=jnp.float32,
    ).astype(out.dtype)


def body(features, weight, grad_out, tile_values, tile_rows, tile_cols, tile_count):
    slots, edge = tile_values.shape[2], tile_values.shape[3]
    width = features.shape[1]
    blocks = lax.axis_size("repl")
    tiles = in_hbm(tile_values.reshape(slots, edge, edge))
    ints = [
        in_hbm(tile_rows.reshape(slots)),
        in_hbm(tile_cols.reshape(slots)),
    ]
    flops = 2 * slots * edge * edge * width
    moved = slots * edge * edge * 2

    spread, *ints = pl.pallas_call(
        spread_kernel,
        out_shape=[
            pltpu.VMEM((blocks, width, edge), jnp.bfloat16),
            pltpu.VMEM((slots,), jnp.int32),
            pltpu.VMEM((slots,), jnp.int32),
        ],
        in_specs=[HBM] * 3,
        out_specs=[VMEM] * 3,
        scratch_shapes=[
            pltpu.VMEM((edge, width), jnp.bfloat16),
            pltpu.SemaphoreType.DMA((3,)),
        ],
        compiler_params=LIMIT,
        name="spread",
    )(in_hbm(grad_out), *ints)
    slab_grads = lax.all_to_all(spread, "repl", 0, 0, tiled=True)
    below = shifted(features, "dom", REACH)
    above = shifted(features, "dom", -REACH)
    lists = pltpu.SMEM((2, slots), jnp.int32)
    extra = [pltpu.VMEM((edge, edge), jnp.bfloat16), pltpu.SemaphoreType.DMA]
    held = pl.pallas_call(
        hold_kernel,
        out_shape=pltpu.VMEM((KEPT, edge, edge), jnp.bfloat16),
        in_specs=[SMEM] * 2 + [HBM],
        out_specs=VMEM,
        scratch_shapes=[lists, pltpu.SemaphoreType.DMA((KEPT,))],
        cost_estimate=pl.CostEstimate(flops=0, bytes_accessed=moved, transcendentals=0),
        compiler_params=LIMIT,
        name="hold",
    )(ints[1], tile_count, tiles)
    packed = pltpu.VMEM((2, edge, width), jnp.bfloat16)
    up, down, ends = pl.pallas_call(
        early_kernel,
        out_shape=[packed, packed, pltpu.VMEM((3, edge, width), jnp.bfloat16)],
        in_specs=[SMEM] * 3 + [HBM] * 2 + [VMEM] * 4,
        out_specs=[VMEM] * 3,
        scratch_shapes=[lists, pltpu.VMEM((3, width, edge), jnp.float32)]
        + extra
        + [pltpu.SemaphoreType.DMA((3,))],
        cost_estimate=pl.CostEstimate(flops=flops, bytes_accessed=moved, transcendentals=0),
        compiler_params=LIMIT,
        name="early",
    )(*ints, tile_count, tiles, in_hbm(features), held, slab_grads, below, above)
    from_above = shifted(down, "dom", -1)
    from_below = shifted(up, "dom", 1)
    cost = pl.CostEstimate(flops=flops, bytes_accessed=moved, transcendentals=0)
    term = pltpu.VMEM((width, edge), jnp.bfloat16)
    sums, far_down, center, far_up = pl.pallas_call(
        middle_kernel,
        out_shape=[
            pltpu.VMEM((blocks, edge, width), jnp.float32),
            term,
            pltpu.VMEM((width, edge), jnp.float32),
            term,
        ],
        in_specs=[SMEM] * 3 + [HBM] + [VMEM] * 2,
        out_specs=[VMEM] * 4,
        scratch_shapes=[
            lists,
            pltpu.VMEM((slots, edge, edge), jnp.bfloat16),
            pltpu.VMEM((blocks + 1, edge, width), jnp.float32),
            pltpu.VMEM((4, width, edge), jnp.float32),
            pltpu.SemaphoreType.DMA((slots,)),
        ],
        cost_estimate=cost,
        compiler_params=LIMIT,
        name="middle",
    )(*ints, tile_count, tiles, slab_grads, ends)
    partial, kept = pl.pallas_call(
        late_kernel,
        out_shape=[
            pltpu.VMEM((blocks, edge, width), jnp.bfloat16),
            pltpu.VMEM((edge, width), jnp.float32),
        ],
        in_specs=[SMEM] * 3 + [HBM] + [VMEM] * 5,
        out_specs=[VMEM] * 2,
        scratch_shapes=[
            lists,
            pltpu.VMEM((2, edge, width), jnp.bfloat16),
            pltpu.VMEM((blocks + 1, edge, width), jnp.float32),
        ]
        + extra,
        cost_estimate=cost,
        compiler_params=LIMIT,
        name="late",
    )(*ints, tile_count, tiles, held, sums, center, from_above, from_below)
    slab_parts = lax.all_to_all(partial, "repl", 0, 0, tiled=True)
    far_from_above = shifted(far_down, "dom", -REACH)
    far_from_below = shifted(far_up, "dom", REACH)
    block = jax.ShapeDtypeStruct((edge, width), jnp.bfloat16)
    projected, kept = pl.pallas_call(
        project_kernel,
        out_shape=[block, pltpu.VMEM((edge, width), jnp.float32)],
        in_specs=[VMEM] * 3,
        out_specs=[VMEM] * 2,
        compiler_params=LIMIT,
        name="project",
    )(slab_parts, weight, kept)
    grad_features = pl.pallas_call(
        features_kernel,
        out_shape=block,
        in_specs=[VMEM] * 4,
        out_specs=VMEM,
        compiler_params=LIMIT,
        name="features",
    )(kept, far_from_above, far_from_below, weight)
    return projected, grad_features


def solution(mesh):
    placed = (
        P(("dom", "repl"), None),
        P(),
        P(("dom", "repl"), None),
        P("dom", "repl", None, None, None),
        P("dom", "repl", None),
        P("dom", "repl", None),
        P("dom", "repl"),
    )
    return jax.shard_map(
        body,
        mesh=mesh,
        in_specs=placed,
        out_specs=(P(("dom", "repl"), None), P(("dom", "repl"), None)),
        check_vma=False,
    )
```

time: 58.4 us -> 59.8 us (1.024)
  waiting for transfers between devices: 15.7 us -> 6.57 us
  starting transfers between devices: 31.4 us -> 37 us
  Pallas kernels: 8.99 us -> 13.7 us
    ppermute x6, starting transfers between devices: 8.51 us -> 14.6 us  [shifted(): return lax.ppermute(array, axis, pairs)]
    ppermute x6, waiting for transfers between devices: 8.55 us -> 2.82 us  [shifted(): return lax.ppermute(array, axis, pairs)]
    all_to_all x1, waiting for transfers between devices: 6.12 us -> 2.71 us  [body(): slab_parts = lax.all_to_all(partial, 'repl', 0, 0, tiled=True)]
    pallas_call x1, Pallas kernels: 1.37 us -> 3.83 us  [body(): pl.pallas_call(middle_kernel, out_shape=[pltpu.VMEM((blocks, edge, width)...]
    pallas_call x2 -> x3, Pallas kernels: 3.97 us -> 5.74 us  [the longest x1 2.4 us: body(): pl.pallas_call(hold_kernel, out_shape=pltpu.VMEM((KEPT, edge, edge), jnp....]
  transfers between devices with their start and end apart: 8 -> 8, of which waited for: 4 -> 3; matrix products, arithmetic and copies ran while one was open for 0% -> 0% of each run, Pallas kernels for 4% -> 12%
where the time goes in v4:
time: 59.8 us; the launch traced here: 58.7 us
  starting transfers between devices  37 us (62%)
  Pallas kernels  13.7 us (23%)
  waiting for transfers between devices  6.57 us (11%)
  between operations  1.4 us (2%)
    all_to_all x1, starting transfers between devices, body(): slab_grads = lax.all_to_all(spread, 'repl', 0, 0, tiled=True)  17.6 us
    ppermute x6, starting transfers between devices, shifted(): return lax.ppermute(array, axis, pairs)  14.6 us
    all_to_all x1, starting transfers between devices, body(): slab_parts = lax.all_to_all(partial, 'repl', 0, 0, tiled=True)  4.82 us
    pallas_call x1, Pallas kernels, body(): pl.pallas_call(middle_kernel, out_shape=[pltpu.VMEM((blocks, edge, width)...  3.83 us
    ppermute x6, waiting for transfers between devices, shifted(): return lax.ppermute(array, axis, pairs)  2.82 us
    all_to_all x1, waiting for transfers between devices, body(): slab_parts = lax.all_to_all(partial, 'repl', 0, 0, tiled=True)  2.71 us
    pallas_call x1, Pallas kernels, body(): pl.pallas_call(late_kernel, out_shape=[pltpu.VMEM((blocks, edge, width),...  2.5 us
    pallas_call x1, Pallas kernels, body(): pl.pallas_call(hold_kernel, out_shape=pltpu.VMEM((KEPT, edge, edge), jnp....  2.4 us
  transfers between devices with their start and end apart: 8, of which 3 were waited for; matrix products, arithmetic and copies ran while one was open for 0% of the time, Pallas kernels for 12%

profile of v4, /device:TPU:1, one launch (start us, length us, event | category | flops | bytes accessed | tf_op | source)
XLA Modules:
  0.0 58.7 jit_solution(11804929516952308062)
XLA Ops:
  0.6 1.7 %spread.1 = (bf16[8,128,256]{2,1,0:T(8,128)(2,1)}, s32[24]{0:T(128)S(1)}, s32[24]{0:T(128)S(1)}) custom-call(bf16[256,128]{1,0:T(8,128)(2,1)} %grads.1, s32[24]{0:T(128)} %bitcast.7, s32[24]{0:T(128)} %bitcast.8), custom_call_target="tpu_custom_call" | custom-call | tf_op jit(solution)/shard_map/spread/pallas_call | solution.py:230
  2.4 17.6 %all-to-all-start = ((bf16[8,128,256]{2,1,0:T(8,128)(2,1)}), bf16[8,128,256]{2,1,0:T(8,128)(2,1)S(1)}, u32[]{:S(2)}, u32[]{:S(2)}) async-start(bf16[8,128,256]{2,1,0:T(8,128)(2,1)} %get-tuple-element.18), calls=%async_computation | async-start | bytes 1048576 | tf_op jit(solution)/shard_map/all_to_all | solution.py:246
  19.9 1.3 %collective-permute-start = (bf16[256,128]{1,0:T(8,128)(2,1)}, bf16[256,128]{1,0:T(8,128)(2,1)S(1)}, u32[]{:S(2)}, u32[]{:S(2)}) collective-permute-start(bf16[256,128]{1,0:T(8,128)(2,1)} %features.2), channel_id=1, source_target_pairs={{0,16},{8,24},{16,32},{24,40},{32,48},{40,56},{48,64},{56,72},{64,... | collective-permute-start | bytes 196616 | tf_op jit(solution)/shard_map/ppermute | solution.py:27
  21.2 1.3 %collective-permute-start.1 = (bf16[256,128]{1,0:T(8,128)(2,1)}, bf16[256,128]{1,0:T(8,128)(2,1)S(1)}, u32[]{:S(2)}, u32[]{:S(2)}) collective-permute-start(bf16[256,128]{1,0:T(8,128)(2,1)} %features.2), channel_id=1, source_target_pairs={{16,0},{24,8},{32,16},{40,24},{48,32},{56,40},{64,48},{72,56},{80,... | collective-permute-start | bytes 196616 | tf_op jit(solution)/shard_map/ppermute | solution.py:27
  23.2 2.4 %hold.1.held = bf16[22,256,256]{2,1,0:T(8,128)(2,1)S(1)} custom-call(s32[24]{0:T(128)S(1)} %get-tuple-element.17.cols, s32[1,1]{1,0:T(1,128)S(6)} %copy.9.count, bf16[24,256,256]{2,1,0:T(8,128)(2,1)} %bitcast.3), custom_call_target="tpu_custom_call" | custom-call | bytes 3145728 | tf_op jit(solution)/shard_map/hold/pallas_call | solution.py:251
  25.6 0.0 collective-permute-done.below
  25.6 2.8 %collective-permute-done.1.above = bf16[256,128]{1,0:T(8,128)(2,1)S(1)} collective-permute-done((bf16[256,128]{1,0:T(8,128)(2,1)}, bf16[256,128]{1,0:T(8,128)(2,1)S(1)}, u32[]{:S(2)}, u32[]{:S(2)}) %collective-permute-start.1) | collective-permute-done | bytes 65568 | tf_op jit(solution)/shard_map/ppermute | solution.py:27
  28.4 1.0 %all-to-all-done.grads = bf16[8,128,256]{2,1,0:T(8,128)(2,1)S(1)} async-done(((bf16[8,128,256]{2,1,0:T(8,128)(2,1)}), bf16[8,128,256]{2,1,0:T(8,128)(2,1)S(1)}, u32[]{:S(2)}, u32[]{:S(2)}) %all-to-all-start) | async-done | bytes 524320 | tf_op jit(solution)/shard_map/all_to_all | solution.py:246
  29.4 1.6 %early.1 = (bf16[2,256,128]{2,1,0:T(8,128)(2,1)S(1)}, bf16[2,256,128]{2,1,0:T(8,128)(2,1)S(1)}, bf16[3,256,128]{2,1,0:T(8,128)(2,1)S(1)}) custom-call(s32[24]{0:T(128)S(1)} %get-tuple-element.16.rows, s32[24]{0:T(128)S(1)} %get-tuple-element.17.cols, s32[1,1]{1,0:T(1,128)S(6)} %copy.9.count, bf16[24,256,256]{2,1,0:T(8,128)(2,1)} %bitcast.4, ...), custom_call_target="tpu_custom_call" | custom-call | flops 402653184 | bytes 3145728 | tf_op jit(solution)/shard_map/early/pallas_call | solution.py:262
  31.0 1.3 %collective-permute-start.2 = (bf16[2,256,128]{2,1,0:T(8,128)(2,1)S(1)}, bf16[2,256,128]{2,1,0:T(8,128)(2,1)S(1)}, u32[]{:S(2)}, u32[]{:S(2)}) collective-permute-start(bf16[2,256,128]{2,1,0:T(8,128)(2,1)S(1)} %get-tuple-element.22), channel_id=1, source_target_pairs={{8,0},{16,8},{24,16},{32,24},{40,32},{48,40},{56,48},{64,56},{72,6... | collective-permute-start | bytes 393224 | tf_op jit(solution)/shard_map/ppermute | solution.py:27
  32.3 4.0 %collective-permute-start.3 = (bf16[2,256,128]{2,1,0:T(8,128)(2,1)S(1)}, bf16[2,256,128]{2,1,0:T(8,128)(2,1)S(1)}, u32[]{:S(2)}, u32[]{:S(2)}) collective-permute-start(bf16[2,256,128]{2,1,0:T(8,128)(2,1)S(1)} %get-tuple-element.23), channel_id=1, source_target_pairs={{0,8},{8,16},{16,24},{24,32},{32,40},{40,48},{48,56},{56,64},{64,7... | collective-permute-start | bytes 393224 | tf_op jit(solution)/shard_map/ppermute | solution.py:27
  36.3 3.8 %middle.1 = (f32[8,256,128]{2,1,0:T(8,128)S(1)}, bf16[128,256]{1,0:T(8,128)(2,1)S(1)}, f32[128,256]{1,0:T(8,128)S(1)}, bf16[128,256]{1,0:T(8,128)(2,1)S(1)}) custom-call(s32[24]{0:T(128)S(1)} %get-tuple-element.16.rows, s32[24]{0:T(128)S(1)} %get-tuple-element.17.cols, s32[1,1]{1,0:T(1,128)S(6)} %copy.9.count, bf16[24,256,256]{2,1,0:T(8,128)(2,1)} %bitcast.5, ...), custom_call_target="tpu_custom_call" | custom-call | flops 402653184 | bytes 3145728 | tf_op jit(solution)/shard_map/middle/pallas_call | solution.py:278
  40.2 0.0 collective-permute-done.2.from_above
  40.2 0.0 collective-permute-done.3.from_below
  40.2 0.0 copy-start
  40.2 2.5 %late.1 = (bf16[8,256,128]{2,1,0:T(8,128)(2,1)}, f32[256,128]{1,0:T(8,128)S(1)}) custom-call(s32[24]{0:T(128)S(1)} %get-tuple-element.16.rows, s32[24]{0:T(128)S(1)} %get-tuple-element.17.cols, s32[1,1]{1,0:T(1,128)S(6)} %copy.9.count, bf16[24,256,256]{2,1,0:T(8,128)(2,1)} %bitcast.6, bf16[22,256,256]{2,1,0:T(8,128)(2,1)S(1)} %hold.1.held, ...), custom_call_target="tpu_custom_call" | custom-call | flops 402653184 | bytes 3145728 | tf_op jit(solution)/shard_map/late/pallas_call | solution.py:299
  42.7 4.8 %all-to-all-start.1 = ((bf16[8,256,128]{2,1,0:T(8,128)(2,1)}), bf16[8,256,128]{2,1,0:T(8,128)(2,1)S(1)}, u32[]{:S(2)}, u32[]{:S(2)}) async-start(bf16[8,256,128]{2,1,0:T(8,128)(2,1)} %get-tuple-element.24), calls=%async_computation.1 | async-start | bytes 1048576 | tf_op jit(solution)/shard_map/all_to_all | solution.py:317
  47.5 1.3 %collective-permute-start.4 = (bf16[128,256]{1,0:T(8,128)(2,1)S(1)}, bf16[128,256]{1,0:T(8,128)(2,1)S(1)}, u32[]{:S(2)}, u32[]{:S(2)}) collective-permute-start(bf16[128,256]{1,0:T(8,128)(2,1)S(1)} %get-tuple-element.28), channel_id=1, source_target_pairs={{16,0},{24,8},{32,16},{40,24},{48,32},{56,40},{64,48},{72,56},{80,... | collective-permute-start | bytes 196616 | tf_op jit(solution)/shard_map/ppermute | solution.py:27
  48.8 5.5 %collective-permute-start.5 = (bf16[128,256]{1,0:T(8,128)(2,1)S(1)}, bf16[128,256]{1,0:T(8,128)(2,1)S(1)}, u32[]{:S(2)}, u32[]{:S(2)}) collective-permute-start(bf16[128,256]{1,0:T(8,128)(2,1)S(1)} %get-tuple-element.29), channel_id=1, source_target_pairs={{0,16},{8,24},{16,32},{24,40},{32,48},{40,56},{48,64},{56,72},{64,... | collective-permute-start | bytes 196616 | tf_op jit(solution)/shard_map/ppermute | solution.py:27
  54.3 2.7 %all-to-all-done.1.parts = bf16[8,256,128]{2,1,0:T(8,128)(2,1)S(1)} async-done(((bf16[8,256,128]{2,1,0:T(8,128)(2,1)}), bf16[8,256,128]{2,1,0:T(8,128)(2,1)S(1)}, u32[]{:S(2)}, u32[]{:S(2)}) %all-to-all-start.1) | async-done | bytes 524320 | tf_op jit(solution)/shard_map/all_to_all | solution.py:317
  57.0 0.8 %project.1 = (bf16[256,128]{1,0:T(8,128)(2,1)}, f32[256,128]{1,0:T(8,128)S(1)}) custom-call(bf16[8,256,128]{2,1,0:T(8,128)(2,1)S(1)} %all-to-all-done.1.parts, bf16[128,128]{1,0:T(8,128)(2,1)S(1)} %copy-done, f32[256,128]{1,0:T(8,128)S(1)} %get-tuple-element.25.kept), custom_call_target="tpu_custom_call" | custom-call | tf_op jit(solution)/shard_map/project/pallas_call | solution.py:321
  57.9 0.0 collective-permute-done.4.from_below
  57.9 0.0 collective-permute-done.5.from_above
  57.9 0.9 %features.3 = bf16[256,128]{1,0:T(8,128)(2,1)} custom-call(f32[256,128]{1,0:T(8,128)S(1)} %get-tuple-element.27.kept, bf16[128,256]{1,0:T(8,128)(2,1)S(1)} %collective-permute-done.4.from_below, bf16[128,256]{1,0:T(8,128)(2,1)S(1)} %collective-permute-done.5.from_above, bf16[128,128]{1,0:T(8,128)(2,1)S(1)} %copy-done), custom_call_target="tpu_custom_call" | custom-call | tf_op jit(solution)/shard_map/features/pallas_call | solution.py:329
  (1 shorter events, 0.0 us)
Async XLA Ops:
  2.4 27.1 %all-to-all-start = ((bf16[8,128,256]{2,1,0:T(8,128)(2,1)}), bf16[8,128,256]{2,1,0:T(8,128)(2,1)S(1)}, u32[]{:S(2)}, u32[]{:S(2)}) async-start(bf16[8,128,256]{2,1,0:T(8,128)(2,1)} %get-tuple-element.18), calls=%async_computation | async-start | bytes 1048576 | tf_op jit(solution)/shard_map/all_to_all | solution.py:246
  19.9 5.6 %collective-permute-start = (bf16[256,128]{1,0:T(8,128)(2,1)}, bf16[256,128]{1,0:T(8,128)(2,1)S(1)}, u32[]{:S(2)}, u32[]{:S(2)}) collective-permute-start(bf16[256,128]{1,0:T(8,128)(2,1)} %features.2), channel_id=1, source_target_pairs={{0,16},{8,24},{16,32},{24,40},{32,48},{40,56},{48,64},{56,72},{64,... | collective-permute-start | bytes 196616 | tf_op jit(solution)/shard_map/ppermute | solution.py:27
  21.2 7.2 %collective-permute-start.1 = (bf16[256,128]{1,0:T(8,128)(2,1)}, bf16[256,128]{1,0:T(8,128)(2,1)S(1)}, u32[]{:S(2)}, u32[]{:S(2)}) collective-permute-start(bf16[256,128]{1,0:T(8,128)(2,1)} %features.2), channel_id=1, source_target_pairs={{16,0},{24,8},{32,16},{40,24},{48,32},{56,40},{64,48},{72,56},{80,... | collective-permute-start | bytes 196616 | tf_op jit(solution)/shard_map/ppermute | solution.py:27
  31.0 9.1 %collective-permute-start.2 = (bf16[2,256,128]{2,1,0:T(8,128)(2,1)S(1)}, bf16[2,256,128]{2,1,0:T(8,128)(2,1)S(1)}, u32[]{:S(2)}, u32[]{:S(2)}) collective-permute-start(bf16[2,256,128]{2,1,0:T(8,128)(2,1)S(1)} %get-tuple-element.22), channel_id=1, source_target_pairs={{8,0},{16,8},{24,16},{32,24},{40,32},{48,40},{56,48},{64,56},{72,6... | collective-permute-start | bytes 393224 | tf_op jit(solution)/shard_map/ppermute | solution.py:27
  32.3 7.9 %collective-permute-start.3 = (bf16[2,256,128]{2,1,0:T(8,128)(2,1)S(1)}, bf16[2,256,128]{2,1,0:T(8,128)(2,1)S(1)}, u32[]{:S(2)}, u32[]{:S(2)}) collective-permute-start(bf16[2,256,128]{2,1,0:T(8,128)(2,1)S(1)} %get-tuple-element.23), channel_id=1, source_target_pairs={{0,8},{8,16},{16,24},{24,32},{32,40},{40,48},{48,56},{56,64},{64,7... | collective-permute-start | bytes 393224 | tf_op jit(solution)/shard_map/ppermute | solution.py:27
  40.2 16.8 %copy-start = (bf16[128,128]{1,0:T(8,128)(2,1)S(1)}, bf16[128,128]{1,0:T(8,128)(2,1)}, u32[]{:S(2)}) copy-start(bf16[128,128]{1,0:T(8,128)(2,1)} %weight.3) | copy-start | bytes 98308
  42.7 14.3 %all-to-all-start.1 = ((bf16[8,256,128]{2,1,0:T(8,128)(2,1)}), bf16[8,256,128]{2,1,0:T(8,128)(2,1)S(1)}, u32[]{:S(2)}, u32[]{:S(2)}) async-start(bf16[8,256,128]{2,1,0:T(8,128)(2,1)} %get-tuple-element.24), calls=%async_computation.1 | async-start | bytes 1048576 | tf_op jit(solution)/shard_map/all_to_all | solution.py:317
  47.5 10.3 %collective-permute-start.4 = (bf16[128,256]{1,0:T(8,128)(2,1)S(1)}, bf16[128,256]{1,0:T(8,128)(2,1)S(1)}, u32[]{:S(2)}, u32[]{:S(2)}) collective-permute-start(bf16[128,256]{1,0:T(8,128)(2,1)S(1)} %get-tuple-element.28), channel_id=1, source_target_pairs={{16,0},{24,8},{32,16},{40,24},{48,32},{56,40},{64,48},{72,56},{80,... | collective-permute-start | bytes 196616 | tf_op jit(solution)/shard_map/ppermute | solution.py:27
  48.8 9.0 %collective-permute-start.5 = (bf16[128,256]{1,0:T(8,128)(2,1)S(1)}, bf16[128,256]{1,0:T(8,128)(2,1)S(1)}, u32[]{:S(2)}, u32[]{:S(2)}) collective-permute-start(bf16[128,256]{1,0:T(8,128)(2,1)S(1)} %get-tuple-element.29), channel_id=1, source_target_pairs={{0,16},{8,24},{16,32},{24,40},{32,48},{40,56},{48,64},{56,72},{64,... | collective-permute-start | bytes 196616 | tf_op jit(solution)/shard_map/ppermute | solution.py:27
